TPU v7x, 512 devices: a whole 4x4x16 slice. The times are simulated.
512 devices in a mesh: kring: 16 (over y_hi, x, core), orb: 32 (over y_lo, z).
Axes of the slice: x: 4, y: 4 (y_hi: 2, y_lo: 2; y = y_hi * 2 + y_lo), z: 16, core: 2. Of those that a mesh axis runs over, the one named last changes fastest.
Arguments:
- tau_slabs: bfloat16 [32, 2, 112, 28672], P('kring', None, None, 'orb'), may hold values from -0.005859375 to 0.005859375
- lambda_slabs: bfloat16 [32, 2, 112, 28672], P('kring', None, None, 'orb'), may hold values from -0.5 to 0.5
- aux_factor: bfloat16 [2, 2, 112, 53760], P(None, None, None, 'orb'), may hold values from -0.375 to 0.375
- transfer_table: int32 [32, 32], replicated, may hold values from 0 to 2, as said below
Outputs:
- gamma_density: float32 [2, 2, 112, 53760], P(None, None, 'kring', 'orb')
Inputs may be any that keep to these rules, and one draw needn't show every extreme that they name: transfer_table[t, u] is the momentum transfer that Tau triple t and Lambda triple u contribute to, or 2 where they share no occupied k-pair; each Tau triple has one or two Lambda partners.
All inputs are finite; a program needn't handle non-finite values.
Results may differ from a plain program's by a relative error of at most 0.0029.
Values may be sent and summed in bfloat16 or wider, within the bound.
No kernel may reach another device: no remote copies, remote signals or barrier semaphores. Data moves between devices by JAX's collectives and lax.ppermute only.
A program may use at most 64 MiB of HBM per device.

v0:
```python
import jax
import jax.numpy as jnp
from jax import lax
from jax.sharding import PartitionSpec as P


def passed_along(value, axis, steps):
    count = lax.axis_size(axis)
    pairs = [(source, (source + steps) % count) for source in range(count)]
    return lax.ppermute(value, axis, pairs)


def local(tau_slabs, lambda_slabs, aux_factor, transfer_table):
    kring_count = lax.axis_size("kring")
    kring_index = lax.axis_index("kring")
    triples = tau_slabs.shape[0]
    virtuals = tau_slabs.shape[2]
    contracted = tau_slabs.shape[3]
    qcount = aux_factor.shape[0]
    lambda_rows = lambda_slabs.reshape(triples * 2 * virtuals, contracted)

    def pair_terms(visiting, lambda_part, anchor):
        tau_rows = visiting.reshape(triples * 2 * virtuals, visiting.shape[3])
        products = lax.dot_general(
            tau_rows, lambda_part, (((1,), (1,)), ((), ())), preferred_element_type=jnp.float32
        )
        products = products.reshape(triples, 2, virtuals, triples, 2, virtuals)
        real_part = products[:, 0, :, :, 0, :] + products[:, 1, :, :, 1, :]
        imag_part = products[:, 1, :, :, 0, :] - products[:, 0, :, :, 1, :]
        stacked = jnp.stack([real_part, imag_part], 0)
        table_rows = lax.dynamic_slice(
            transfer_table, (anchor * triples, kring_index * triples), (triples, triples)
        )
        weights = (table_rows[None] == jnp.arange(qcount, dtype=jnp.int32)[:, None, None]).astype(
            jnp.float32
        )
        return jnp.einsum("qtu,rtaud->qrad", weights, stacked, precision=lax.Precision.HIGHEST)

    totals = pair_terms(tau_slabs, lambda_rows, kring_index)

    def advance(position, state_pair):
        visiting, running = state_pair
        visiting = passed_along(visiting, "kring", 1)
        anchor = (kring_index - position) % kring_count
        return (visiting, running + pair_terms(visiting, lambda_rows, anchor))

    visiting, totals = lax.fori_loop(1, kring_count, advance, (tau_slabs, totals))
    rows_owned = virtuals // kring_count
    summed = lax.psum(totals, ("kring", "orb"))
    owned = lax.dynamic_slice_in_dim(summed, kring_index * rows_owned, rows_owned, 2)
    density = owned.astype(jnp.bfloat16)
    upper = jnp.concatenate([density[:, 0], -density[:, 1]], 2)
    lower = jnp.concatenate([density[:, 1], density[:, 0]], 2)
    blocked = jnp.concatenate([upper, lower], 1)
    factors = aux_factor.reshape(qcount, 2 * virtuals, aux_factor.shape[3])
    gamma_block = jnp.einsum("qrd,qdc->qrc", blocked, factors, preferred_element_type=jnp.float32)
    return gamma_block.reshape(qcount, 2, rows_owned, aux_factor.shape[3])


def solution(mesh):
    in_specs = (
        P("kring", None, None, "orb"),
        P("kring", None, None, "orb"),
        P(None, None, None, "orb"),
        P(),
    )
    out_specs = P(None, None, "kring", "orb")
    return jax.shard_map(local, mesh=mesh, in_specs=in_specs, out_specs=out_specs, check_vma=False)
```

profile of v0, /device:TPU:1, one launch (start us, length us, event | category | flops | bytes accessed | tf_op | source)
XLA Modules:
  0.0 423.6 jit_solution(3043374471232243517)
XLA Ops:
  2.0 1.8 fusion.11
  4.9 300.3 %while.17 = (s32[]{:T(128)}, bf16[2,2,112,896]{3,2,1,0:T(8,128)(2,1)S(1)}, f32[2,2,112,112]{3,0,2,1:T(2,128)S(1)}, s32[]{:T(128)}, s32[32,32]{1,0:T(8,128)}, /*i...) while((s32[]{:T(128)}, ...), condition=%wide.region_1.2_spmd, body=%wide.region_0.1_spmd.sunk | while | flops 362320896 | bytes 10035584 | solution.py:47
  4.9 4.5 %collective-permute-start = (bf16[2,2,112,896]{3,2,1,0:T(8,128)(2,1)S(1)}, bf16[2,2,112,896]{3,2,1,0:T(8,128)(2,1)S(1)}, u32[]{:S(2)}, u32[]{:S(2)}) collective-permute-start(bf16[2,2,112,896]{3,2,1,0:T(8,128)(2,1)S(1)} %get-tuple-element.243), channel_id=1, source_target_pairs={{0,32},{32,64},{64,96},{96,128},{128,160},{160,192},{192,224},{224... | collective-permute-start | bytes 2408456 | tf_op jit(solution)/shard_map/while/body/eval_jaxpr/ppermute | solution.py:10
  10.3 8.3 %collective-permute-done = bf16[2,2,112,896]{3,2,1,0:T(8,128)(2,1)S(1)} collective-permute-done((bf16[2,2,112,896]{3,2,1,0:T(8,128)(2,1)S(1)}, bf16[2,2,112,896]{3,2,1,0:T(8,128)(2,1)S(1)}, u32[]{:S(2)}, u32[]{:S(2)}) %collective-permute-start) | collective-permute-done | bytes 802848 | tf_op jit(solution)/shard_map/while/body/eval_jaxpr/ppermute | solution.py:10
  18.6 1.8 fusion.46
  21.9 4.4 %collective-permute-start = (bf16[2,2,112,896]{3,2,1,0:T(8,128)(2,1)S(1)}, bf16[2,2,112,896]{3,2,1,0:T(8,128)(2,1)S(1)}, u32[]{:S(2)}, u32[]{:S(2)}) collective-permute-start(bf16[2,2,112,896]{3,2,1,0:T(8,128)(2,1)S(1)} %get-tuple-element.243), channel_id=1, source_target_pairs={{0,32},{32,64},{64,96},{96,128},{128,160},{160,192},{192,224},{224... | collective-permute-start | bytes 2408456 | tf_op jit(solution)/shard_map/while/body/eval_jaxpr/ppermute | solution.py:10
  27.1 8.9 %collective-permute-done = bf16[2,2,112,896]{3,2,1,0:T(8,128)(2,1)S(1)} collective-permute-done((bf16[2,2,112,896]{3,2,1,0:T(8,128)(2,1)S(1)}, bf16[2,2,112,896]{3,2,1,0:T(8,128)(2,1)S(1)}, u32[]{:S(2)}, u32[]{:S(2)}) %collective-permute-start) | collective-permute-done | bytes 802848 | tf_op jit(solution)/shard_map/while/body/eval_jaxpr/ppermute | solution.py:10
  36.0 1.8 fusion.46
  39.3 3.8 collective-permute-start
  43.9 12.5 %collective-permute-done = bf16[2,2,112,896]{3,2,1,0:T(8,128)(2,1)S(1)} collective-permute-done((bf16[2,2,112,896]{3,2,1,0:T(8,128)(2,1)S(1)}, bf16[2,2,112,896]{3,2,1,0:T(8,128)(2,1)S(1)}, u32[]{:S(2)}, u32[]{:S(2)}) %collective-permute-start) | collective-permute-done | bytes 802848 | tf_op jit(solution)/shard_map/while/body/eval_jaxpr/ppermute | solution.py:10
  56.4 1.8 fusion.46
  59.8 1.9 collective-permute-start
  62.5 14.4 %collective-permute-done = bf16[2,2,112,896]{3,2,1,0:T(8,128)(2,1)S(1)} collective-permute-done((bf16[2,2,112,896]{3,2,1,0:T(8,128)(2,1)S(1)}, bf16[2,2,112,896]{3,2,1,0:T(8,128)(2,1)S(1)}, u32[]{:S(2)}, u32[]{:S(2)}) %collective-permute-start) | collective-permute-done | bytes 802848 | tf_op jit(solution)/shard_map/while/body/eval_jaxpr/ppermute | solution.py:10
  76.9 1.8 fusion.46
  80.2 1.9 collective-permute-start
  82.9 14.4 %collective-permute-done = bf16[2,2,112,896]{3,2,1,0:T(8,128)(2,1)S(1)} collective-permute-done((bf16[2,2,112,896]{3,2,1,0:T(8,128)(2,1)S(1)}, bf16[2,2,112,896]{3,2,1,0:T(8,128)(2,1)S(1)}, u32[]{:S(2)}, u32[]{:S(2)}) %collective-permute-start) | collective-permute-done | bytes 802848 | tf_op jit(solution)/shard_map/while/body/eval_jaxpr/ppermute | solution.py:10
  97.3 1.8 fusion.46
  100.7 1.9 collective-permute-start
  103.4 14.4 %collective-permute-done = bf16[2,2,112,896]{3,2,1,0:T(8,128)(2,1)S(1)} collective-permute-done((bf16[2,2,112,896]{3,2,1,0:T(8,128)(2,1)S(1)}, bf16[2,2,112,896]{3,2,1,0:T(8,128)(2,1)S(1)}, u32[]{:S(2)}, u32[]{:S(2)}) %collective-permute-start) | collective-permute-done | bytes 802848 | tf_op jit(solution)/shard_map/while/body/eval_jaxpr/ppermute | solution.py:10
  117.8 1.8 fusion.46
  121.1 1.9 collective-permute-start
  123.8 14.4 %collective-permute-done = bf16[2,2,112,896]{3,2,1,0:T(8,128)(2,1)S(1)} collective-permute-done((bf16[2,2,112,896]{3,2,1,0:T(8,128)(2,1)S(1)}, bf16[2,2,112,896]{3,2,1,0:T(8,128)(2,1)S(1)}, u32[]{:S(2)}, u32[]{:S(2)}) %collective-permute-start) | collective-permute-done | bytes 802848 | tf_op jit(solution)/shard_map/while/body/eval_jaxpr/ppermute | solution.py:10
  138.2 1.8 fusion.46
  141.6 1.9 collective-permute-start
  144.3 14.4 %collective-permute-done = bf16[2,2,112,896]{3,2,1,0:T(8,128)(2,1)S(1)} collective-permute-done((bf16[2,2,112,896]{3,2,1,0:T(8,128)(2,1)S(1)}, bf16[2,2,112,896]{3,2,1,0:T(8,128)(2,1)S(1)}, u32[]{:S(2)}, u32[]{:S(2)}) %collective-permute-start) | collective-permute-done | bytes 802848 | tf_op jit(solution)/shard_map/while/body/eval_jaxpr/ppermute | solution.py:10
  158.7 1.8 fusion.46
  162.1 1.9 collective-permute-start
  164.8 14.4 %collective-permute-done = bf16[2,2,112,896]{3,2,1,0:T(8,128)(2,1)S(1)} collective-permute-done((bf16[2,2,112,896]{3,2,1,0:T(8,128)(2,1)S(1)}, bf16[2,2,112,896]{3,2,1,0:T(8,128)(2,1)S(1)}, u32[]{:S(2)}, u32[]{:S(2)}) %collective-permute-start) | collective-permute-done | bytes 802848 | tf_op jit(solution)/shard_map/while/body/eval_jaxpr/ppermute | solution.py:10
  179.2 1.8 fusion.46
  182.5 1.9 collective-permute-start
  185.2 14.4 %collective-permute-done = bf16[2,2,112,896]{3,2,1,0:T(8,128)(2,1)S(1)} collective-permute-done((bf16[2,2,112,896]{3,2,1,0:T(8,128)(2,1)S(1)}, bf16[2,2,112,896]{3,2,1,0:T(8,128)(2,1)S(1)}, u32[]{:S(2)}, u32[]{:S(2)}) %collective-permute-start) | collective-permute-done | bytes 802848 | tf_op jit(solution)/shard_map/while/body/eval_jaxpr/ppermute | solution.py:10
  199.6 1.8 fusion.46
  203.0 1.9 collective-permute-start
  205.7 14.4 %collective-permute-done = bf16[2,2,112,896]{3,2,1,0:T(8,128)(2,1)S(1)} collective-permute-done((bf16[2,2,112,896]{3,2,1,0:T(8,128)(2,1)S(1)}, bf16[2,2,112,896]{3,2,1,0:T(8,128)(2,1)S(1)}, u32[]{:S(2)}, u32[]{:S(2)}) %collective-permute-start) | collective-permute-done | bytes 802848 | tf_op jit(solution)/shard_map/while/body/eval_jaxpr/ppermute | solution.py:10
  220.1 1.8 fusion.46
  223.4 1.9 collective-permute-start
  226.2 14.4 %collective-permute-done = bf16[2,2,112,896]{3,2,1,0:T(8,128)(2,1)S(1)} collective-permute-done((bf16[2,2,112,896]{3,2,1,0:T(8,128)(2,1)S(1)}, bf16[2,2,112,896]{3,2,1,0:T(8,128)(2,1)S(1)}, u32[]{:S(2)}, u32[]{:S(2)}) %collective-permute-start) | collective-permute-done | bytes 802848 | tf_op jit(solution)/shard_map/while/body/eval_jaxpr/ppermute | solution.py:10
  240.6 1.8 fusion.46
  243.9 1.9 collective-permute-start
  246.6 14.4 %collective-permute-done = bf16[2,2,112,896]{3,2,1,0:T(8,128)(2,1)S(1)} collective-permute-done((bf16[2,2,112,896]{3,2,1,0:T(8,128)(2,1)S(1)}, bf16[2,2,112,896]{3,2,1,0:T(8,128)(2,1)S(1)}, u32[]{:S(2)}, u32[]{:S(2)}) %collective-permute-start) | collective-permute-done | bytes 802848 | tf_op jit(solution)/shard_map/while/body/eval_jaxpr/ppermute | solution.py:10
  261.0 1.8 fusion.46
  264.4 1.9 collective-permute-start
  267.1 14.4 %collective-permute-done = bf16[2,2,112,896]{3,2,1,0:T(8,128)(2,1)S(1)} collective-permute-done((bf16[2,2,112,896]{3,2,1,0:T(8,128)(2,1)S(1)}, bf16[2,2,112,896]{3,2,1,0:T(8,128)(2,1)S(1)}, u32[]{:S(2)}, u32[]{:S(2)}) %collective-permute-start) | collective-permute-done | bytes 802848 | tf_op jit(solution)/shard_map/while/body/eval_jaxpr/ppermute | solution.py:10
  281.5 1.8 fusion.46
  284.8 1.9 collective-permute-start
  287.5 14.4 %collective-permute-done = bf16[2,2,112,896]{3,2,1,0:T(8,128)(2,1)S(1)} collective-permute-done((bf16[2,2,112,896]{3,2,1,0:T(8,128)(2,1)S(1)}, bf16[2,2,112,896]{3,2,1,0:T(8,128)(2,1)S(1)}, u32[]{:S(2)}, u32[]{:S(2)}) %collective-permute-start) | collective-permute-done | bytes 802848 | tf_op jit(solution)/shard_map/while/body/eval_jaxpr/ppermute | solution.py:10
  301.9 1.8 fusion.46
  305.3 116.9 %all-reduce.1 = bf16[2,2,112,112]{3,2,0,1:T(8,128)(2,1)S(1)} all-reduce(f32[2,2,112,112]{3,2,0,1:T(8,128)S(1)} %copy.19), channel_id=1, replica_groups=mesh['kring'=16,'orb'=32] {'kring','orb'}, use_global_device_ids=true, to_apply=%region_2.3 | all-reduce | flops 50176 | bytes 301056 | tf_op jit(solution)/shard_map/psum | solution.py:49
  (105 shorter events, 38.5 us)
Async XLA Ops:
  0.0 422.3 %copy-start = (bf16[2,2,112,1680]{3,2,1,0:T(8,128)(2,1)S(1)}, bf16[2,2,112,1680]{3,2,1,0:T(8,128)(2,1)}, u32[]{:S(2)}) copy-start(bf16[2,2,112,1680]{3,2,1,0:T(8,128)(2,1)} %param.8) | copy-start | bytes 4515844
  4.9 13.6 %collective-permute-start = (bf16[2,2,112,896]{3,2,1,0:T(8,128)(2,1)S(1)}, bf16[2,2,112,896]{3,2,1,0:T(8,128)(2,1)S(1)}, u32[]{:S(2)}, u32[]{:S(2)}) collective-permute-start(bf16[2,2,112,896]{3,2,1,0:T(8,128)(2,1)S(1)} %get-tuple-element.243), channel_id=1, source_target_pairs={{0,32},{32,64},{64,96},{96,128},{128,160},{160,192},{192,224},{224... | collective-permute-start | bytes 2408456 | tf_op jit(solution)/shard_map/while/body/eval_jaxpr/ppermute | solution.py:10
  21.9 14.1 %collective-permute-start = (bf16[2,2,112,896]{3,2,1,0:T(8,128)(2,1)S(1)}, bf16[2,2,112,896]{3,2,1,0:T(8,128)(2,1)S(1)}, u32[]{:S(2)}, u32[]{:S(2)}) collective-permute-start(bf16[2,2,112,896]{3,2,1,0:T(8,128)(2,1)S(1)} %get-tuple-element.243), channel_id=1, source_target_pairs={{0,32},{32,64},{64,96},{96,128},{128,160},{160,192},{192,224},{224... | collective-permute-start | bytes 2408456 | tf_op jit(solution)/shard_map/while/body/eval_jaxpr/ppermute | solution.py:10
  39.3 17.1 %collective-permute-start = (bf16[2,2,112,896]{3,2,1,0:T(8,128)(2,1)S(1)}, bf16[2,2,112,896]{3,2,1,0:T(8,128)(2,1)S(1)}, u32[]{:S(2)}, u32[]{:S(2)}) collective-permute-start(bf16[2,2,112,896]{3,2,1,0:T(8,128)(2,1)S(1)} %get-tuple-element.243), channel_id=1, source_target_pairs={{0,32},{32,64},{64,96},{96,128},{128,160},{160,192},{192,224},{224... | collective-permute-start | bytes 2408456 | tf_op jit(solution)/shard_map/while/body/eval_jaxpr/ppermute | solution.py:10
  59.8 17.1 %collective-permute-start = (bf16[2,2,112,896]{3,2,1,0:T(8,128)(2,1)S(1)}, bf16[2,2,112,896]{3,2,1,0:T(8,128)(2,1)S(1)}, u32[]{:S(2)}, u32[]{:S(2)}) collective-permute-start(bf16[2,2,112,896]{3,2,1,0:T(8,128)(2,1)S(1)} %get-tuple-element.243), channel_id=1, source_target_pairs={{0,32},{32,64},{64,96},{96,128},{128,160},{160,192},{192,224},{224... | collective-permute-start | bytes 2408456 | tf_op jit(solution)/shard_map/while/body/eval_jaxpr/ppermute | solution.py:10
  80.2 17.1 %collective-permute-start = (bf16[2,2,112,896]{3,2,1,0:T(8,128)(2,1)S(1)}, bf16[2,2,112,896]{3,2,1,0:T(8,128)(2,1)S(1)}, u32[]{:S(2)}, u32[]{:S(2)}) collective-permute-start(bf16[2,2,112,896]{3,2,1,0:T(8,128)(2,1)S(1)} %get-tuple-element.243), channel_id=1, source_target_pairs={{0,32},{32,64},{64,96},{96,128},{128,160},{160,192},{192,224},{224... | collective-permute-start | bytes 2408456 | tf_op jit(solution)/shard_map/while/body/eval_jaxpr/ppermute | solution.py:10
  100.7 17.1 %collective-permute-start = (bf16[2,2,112,896]{3,2,1,0:T(8,128)(2,1)S(1)}, bf16[2,2,112,896]{3,2,1,0:T(8,128)(2,1)S(1)}, u32[]{:S(2)}, u32[]{:S(2)}) collective-permute-start(bf16[2,2,112,896]{3,2,1,0:T(8,128)(2,1)S(1)} %get-tuple-element.243), channel_id=1, source_target_pairs={{0,32},{32,64},{64,96},{96,128},{128,160},{160,192},{192,224},{224... | collective-permute-start | bytes 2408456 | tf_op jit(solution)/shard_map/while/body/eval_jaxpr/ppermute | solution.py:10
  121.1 17.1 %collective-permute-start = (bf16[2,2,112,896]{3,2,1,0:T(8,128)(2,1)S(1)}, bf16[2,2,112,896]{3,2,1,0:T(8,128)(2,1)S(1)}, u32[]{:S(2)}, u32[]{:S(2)}) collective-permute-start(bf16[2,2,112,896]{3,2,1,0:T(8,128)(2,1)S(1)} %get-tuple-element.243), channel_id=1, source_target_pairs={{0,32},{32,64},{64,96},{96,128},{128,160},{160,192},{192,224},{224... | collective-permute-start | bytes 2408456 | tf_op jit(solution)/shard_map/while/body/eval_jaxpr/ppermute | solution.py:10
  141.6 17.1 %collective-permute-start = (bf16[2,2,112,896]{3,2,1,0:T(8,128)(2,1)S(1)}, bf16[2,2,112,896]{3,2,1,0:T(8,128)(2,1)S(1)}, u32[]{:S(2)}, u32[]{:S(2)}) collective-permute-start(bf16[2,2,112,896]{3,2,1,0:T(8,128)(2,1)S(1)} %get-tuple-element.243), channel_id=1, source_target_pairs={{0,32},{32,64},{64,96},{96,128},{128,160},{160,192},{192,224},{224... | collective-permute-start | bytes 2408456 | tf_op jit(solution)/shard_map/while/body/eval_jaxpr/ppermute | solution.py:10
  162.1 17.1 %collective-permute-start = (bf16[2,2,112,896]{3,2,1,0:T(8,128)(2,1)S(1)}, bf16[2,2,112,896]{3,2,1,0:T(8,128)(2,1)S(1)}, u32[]{:S(2)}, u32[]{:S(2)}) collective-permute-start(bf16[2,2,112,896]{3,2,1,0:T(8,128)(2,1)S(1)} %get-tuple-element.243), channel_id=1, source_target_pairs={{0,32},{32,64},{64,96},{96,128},{128,160},{160,192},{192,224},{224... | collective-permute-start | bytes 2408456 | tf_op jit(solution)/shard_map/while/body/eval_jaxpr/ppermute | solution.py:10
  182.5 17.1 %collective-permute-start = (bf16[2,2,112,896]{3,2,1,0:T(8,128)(2,1)S(1)}, bf16[2,2,112,896]{3,2,1,0:T(8,128)(2,1)S(1)}, u32[]{:S(2)}, u32[]{:S(2)}) collective-permute-start(bf16[2,2,112,896]{3,2,1,0:T(8,128)(2,1)S(1)} %get-tuple-element.243), channel_id=1, source_target_pairs={{0,32},{32,64},{64,96},{96,128},{128,160},{160,192},{192,224},{224... | collective-permute-start | bytes 2408456 | tf_op jit(solution)/shard_map/while/body/eval_jaxpr/ppermute | solution.py:10
  203.0 17.1 %collective-permute-start = (bf16[2,2,112,896]{3,2,1,0:T(8,128)(2,1)S(1)}, bf16[2,2,112,896]{3,2,1,0:T(8,128)(2,1)S(1)}, u32[]{:S(2)}, u32[]{:S(2)}) collective-permute-start(bf16[2,2,112,896]{3,2,1,0:T(8,128)(2,1)S(1)} %get-tuple-element.243), channel_id=1, source_target_pairs={{0,32},{32,64},{64,96},{96,128},{128,160},{160,192},{192,224},{224... | collective-permute-start | bytes 2408456 | tf_op jit(solution)/shard_map/while/body/eval_jaxpr/ppermute | solution.py:10
  223.4 17.1 %collective-permute-start = (bf16[2,2,112,896]{3,2,1,0:T(8,128)(2,1)S(1)}, bf16[2,2,112,896]{3,2,1,0:T(8,128)(2,1)S(1)}, u32[]{:S(2)}, u32[]{:S(2)}) collective-permute-start(bf16[2,2,112,896]{3,2,1,0:T(8,128)(2,1)S(1)} %get-tuple-element.243), channel_id=1, source_target_pairs={{0,32},{32,64},{64,96},{96,128},{128,160},{160,192},{192,224},{224... | collective-permute-start | bytes 2408456 | tf_op jit(solution)/shard_map/while/body/eval_jaxpr/ppermute | solution.py:10
  243.9 17.1 %collective-permute-start = (bf16[2,2,112,896]{3,2,1,0:T(8,128)(2,1)S(1)}, bf16[2,2,112,896]{3,2,1,0:T(8,128)(2,1)S(1)}, u32[]{:S(2)}, u32[]{:S(2)}) collective-permute-start(bf16[2,2,112,896]{3,2,1,0:T(8,128)(2,1)S(1)} %get-tuple-element.243), channel_id=1, source_target_pairs={{0,32},{32,64},{64,96},{96,128},{128,160},{160,192},{192,224},{224... | collective-permute-start | bytes 2408456 | tf_op jit(solution)/shard_map/while/body/eval_jaxpr/ppermute | solution.py:10
  264.4 17.1 %collective-permute-start = (bf16[2,2,112,896]{3,2,1,0:T(8,128)(2,1)S(1)}, bf16[2,2,112,896]{3,2,1,0:T(8,128)(2,1)S(1)}, u32[]{:S(2)}, u32[]{:S(2)}) collective-permute-start(bf16[2,2,112,896]{3,2,1,0:T(8,128)(2,1)S(1)} %get-tuple-element.243), channel_id=1, source_target_pairs={{0,32},{32,64},{64,96},{96,128},{128,160},{160,192},{192,224},{224... | collective-permute-start | bytes 2408456 | tf_op jit(solution)/shard_map/while/body/eval_jaxpr/ppermute | solution.py:10
  284.8 17.1 %collective-permute-start = (bf16[2,2,112,896]{3,2,1,0:T(8,128)(2,1)S(1)}, bf16[2,2,112,896]{3,2,1,0:T(8,128)(2,1)S(1)}, u32[]{:S(2)}, u32[]{:S(2)}) collective-permute-start(bf16[2,2,112,896]{3,2,1,0:T(8,128)(2,1)S(1)} %get-tuple-element.243), channel_id=1, source_target_pairs={{0,32},{32,64},{64,96},{96,128},{128,160},{160,192},{192,224},{224... | collective-permute-start | bytes 2408456 | tf_op jit(solution)/shard_map/while/body/eval_jaxpr/ppermute | solution.py:10
where the time goes:
time: 425 us; the launch traced here: 424 us
  waiting for transfers between devices  202 us (48%)
  blocking collectives  117 us (28%)
  matrix products  50.5 us (12%)
  starting transfers between devices  35.7 us (8%)
  local copies, waits for them, and re-layouts  15.5 us (4%)
    ppermute x15, waiting for transfers between devices, passed_along(): return lax.ppermute(value, axis, pairs)  202 us
    psum x1, blocking collectives, local(): summed = lax.psum(totals, ('kring', 'orb'))  117 us
    ppermute x15, starting transfers between devices, passed_along(): return lax.ppermute(value, axis, pairs)  35.7 us
    dot_general x16, matrix products, pair_terms(): lax.dot_general(tau_rows, lambda_part, (((1,), (1,)), ((), ())), preferre...  28.9 us
    dot_general x16, matrix products, pair_terms(): jnp.einsum('qtu,rtaud->qrad', weights, stacked, precision=lax.Precision.H...  21.2 us
    dynamic_slice x16, local copies, waits for them, and re-layouts, pair_terms(): lax.dynamic_slice(transfer_table, (anchor * triples, kring_index * triple...  12.3 us
  transfers between devices with their start and end apart: 15, of which 15 were waited for; matrix products, arithmetic and copies ran while one was open for 3% of the time, Pallas kernels for 0%

commit v1 on v0

v1 whole, which is shorter than its diff:
```python
import jax
import jax.numpy as jnp
from jax import lax
from jax.experimental import pallas as pl
from jax.experimental.pallas import tpu as pltpu
from jax.sharding import PartitionSpec as P

LANES = 128
SUBLANES = 8


def partner_slots(table, shape):
    none = 2
    column = lax.broadcasted_iota(jnp.int32, table.shape, 1)
    used = table != none
    first = jnp.min(jnp.where(used, column, table.shape[1] - 1), 1, keepdims=True)
    last = jnp.max(jnp.where(used, column, 0), 1, keepdims=True)
    first_q = jnp.sum(jnp.where(column == first, table, 0), 1, keepdims=True)
    last_q = jnp.sum(jnp.where(column == last, table, 0), 1, keepdims=True)
    last_q = jnp.where(last == first, none, last_q)
    place = lax.broadcasted_iota(jnp.int32, shape, 1)
    return jnp.where(
        place == 0, first, jnp.where(place == 1, last, jnp.where(place == 2, first_q, last_q))
    )


def pack_kernel(
    tau_ref, lambda_ref, table_ref, packed_ref, slots_ref, both, turned, table_here, slots_here, arrived, left
):
    rows, contracted = tau_ref.shape
    tiles = contracted // LANES
    table_copy = pltpu.make_async_copy(table_ref, table_here, arrived.at[2 * tiles])
    table_copy.start()
    incoming = []
    for tile in range(tiles):
        lanes = pl.ds(tile * LANES, LANES)
        for part, source in enumerate((tau_ref, lambda_ref)):
            incoming.append(
                pltpu.make_async_copy(
                    source.at[:, lanes],
                    both.at[tile, pl.ds(part * rows, rows)],
                    arrived.at[2 * tile + part],
                )
            )
    for copy in incoming:
        copy.start()
    table_copy.wait()
    slots_here[...] = partner_slots(table_here[...], slots_here.shape)
    slots_copy = pltpu.make_async_copy(slots_here, slots_ref, left.at[tiles])
    slots_copy.start()
    outgoing = [slots_copy]
    for tile in range(tiles):
        incoming[2 * tile].wait()
        incoming[2 * tile + 1].wait()
        turned[tile] = both[tile].T
        copy = pltpu.make_async_copy(
            turned.at[tile], packed_ref.at[pl.ds(tile * LANES, LANES)], left.at[tile]
        )
        copy.start()
        outgoing.append(copy)
    for copy in outgoing:
        copy.wait()


def pack(tau_rows, lambda_rows, table):
    rows, contracted = tau_rows.shape
    tiles = contracted // LANES
    return pl.pallas_call(
        pack_kernel,
        out_shape=(
            jax.ShapeDtypeStruct((contracted, 2 * rows), jnp.bfloat16),
            jax.ShapeDtypeStruct((table.shape[0], LANES), jnp.int32),
        ),
        in_specs=[pl.BlockSpec(memory_space=pltpu.HBM)] * 3,
        out_specs=(pl.BlockSpec(memory_space=pltpu.HBM),) * 2,
        scratch_shapes=[
            pltpu.VMEM((tiles, 2 * rows, LANES), jnp.bfloat16),
            pltpu.VMEM((tiles, LANES, 2 * rows), jnp.bfloat16),
            pltpu.VMEM(table.shape, jnp.int32),
            pltpu.VMEM((table.shape[0], LANES), jnp.int32),
            pltpu.SemaphoreType.DMA((2 * tiles + 1,)),
            pltpu.SemaphoreType.DMA((tiles + 1,)),
        ],
        compiler_params=pltpu.CompilerParams(vmem_limit_bytes=56 * 2**20),
        name="pack",
    )(tau_rows, lambda_rows, table)


def pair_kernel(
    virtuals, slots_ref, packed_ref, out_ref, tau_part, lambda_part, chosen, slots, arrived
):
    slots_copy = pltpu.make_async_copy(slots_ref, slots, arrived)
    slots_copy.start()
    groups, depth, width = packed_ref.shape
    triples = 2 * groups
    slot_rows = tau_part.shape[1]
    qcount = 2
    half = width // 2
    fill = jnp.zeros((slot_rows - depth, half), jnp.float32)
    lane_fill = jnp.zeros((slot_rows, LANES - virtuals), jnp.bfloat16)
    for group in range(groups):
        block = packed_ref[group].astype(jnp.float32)
        tau_block = jnp.concatenate([block[:, :half], fill], 0).astype(jnp.bfloat16)
        lambda_block = jnp.concatenate([block[:, half:], fill], 0).astype(jnp.bfloat16)
        for local_triple in range(2):
            start = local_triple * 2 * virtuals
            tau_part[2 * group + local_triple] = tau_block[:, start : start + 2 * virtuals]
            lambda_part[2 * group + local_triple] = jnp.concatenate(
                [
                    lambda_block[:, start : start + virtuals],
                    lane_fill,
                    lambda_block[:, start + virtuals : start + 2 * virtuals],
                    lane_fill,
                ],
                1,
            )

    slots_copy.wait()

    def choose(slot, triple):
        value = lambda_part[slots[triple, slot]]
        transfer = slots[triple, 2 + slot]
        for q in range(qcount):
            chosen[slot, triple, :, q * 2 * LANES : (q + 1) * 2 * LANES] = jnp.where(
                transfer == q, value, jnp.zeros_like(value)
            )

    for triple in range(triples):
        choose(0, triple)
        choose(1, triple)
    tau_all = tau_part[...].reshape(triples * slot_rows, 2 * virtuals)
    total = jnp.zeros((2 * virtuals, qcount * 2 * LANES), jnp.float32)
    for slot in range(2):
        total += lax.dot_general(
            tau_all,
            chosen[slot].reshape(triples * slot_rows, qcount * 2 * LANES),
            (((0,), (0,)), ((), ())),
            preferred_element_type=jnp.float32,
        )
    owned = virtuals // groups
    blank = jnp.zeros((SUBLANES - owned, LANES), jnp.float32)
    for q in range(qcount):
        lane = q * 2 * LANES
        real_lambda = total[:, lane : lane + LANES]
        imag_lambda = total[:, lane + LANES : lane + 2 * LANES]
        real_part = real_lambda[:virtuals] + imag_lambda[virtuals:]
        imag_part = real_lambda[virtuals:] - imag_lambda[:virtuals]
        for place, part in ((2 * q, real_part), (2 * q + 1, imag_part)):
            for group in range(groups):
                out_ref[group, place * SUBLANES : (place + 1) * SUBLANES] = jnp.concatenate(
                    [part[group * owned : (group + 1) * owned], blank], 0
                )


def pair_terms(slots, packed, virtuals):
    groups, depth, width = packed.shape
    slot_rows = -(-depth // 16) * 16
    triples = 2 * groups
    return pl.pallas_call(
        lambda *refs: pair_kernel(virtuals, *refs),
        out_shape=jax.ShapeDtypeStruct((groups, 4 * SUBLANES, LANES), jnp.float32),
        in_specs=[pl.BlockSpec(memory_space=pl.ANY), pl.BlockSpec(memory_space=pltpu.VMEM)],
        out_specs=pl.BlockSpec(memory_space=pltpu.VMEM),
        scratch_shapes=[
            pltpu.VMEM((triples, slot_rows, 2 * virtuals), jnp.bfloat16),
            pltpu.VMEM((triples, slot_rows, 2 * LANES), jnp.bfloat16),
            pltpu.VMEM((2, triples, slot_rows, 4 * LANES), jnp.bfloat16),
            pltpu.SMEM(slots.shape, jnp.int32),
            pltpu.SemaphoreType.DMA,
        ],
        compiler_params=pltpu.CompilerParams(vmem_limit_bytes=40 * 2**20),
        name="pairs",
    )(slots, packed)


def factor_kernel(far, parts_ref, factors_ref, out_ref):
    qcount, depth, _ = factors_ref.shape
    owned = out_ref.shape[1]
    virtuals = depth // 2
    for q in range(qcount):
        density = []
        for component in range(2):
            total = parts_ref[q * far * 2 + component]
            for step in range(1, far):
                total += parts_ref[(q * far + step) * 2 + component]
            density.append(total[:, :virtuals].astype(jnp.bfloat16).astype(jnp.float32))
        real, imag = density
        upper = jnp.concatenate([real, -imag], 1)
        lower = jnp.concatenate([imag, real], 1)
        rows = jnp.concatenate([upper, lower], 0).astype(jnp.bfloat16)
        gamma = jnp.dot(rows, factors_ref[q], preferred_element_type=jnp.float32)
        for row in range(owned):
            out_ref[q, row] = jnp.concatenate(
                [gamma[row : row + 1], gamma[SUBLANES + row : SUBLANES + row + 1]], 0
            )


def factor_product(parts, factors, owned, far):
    qcount, _, columns = factors.shape
    return pl.pallas_call(
        lambda *refs: factor_kernel(far, *refs),
        out_shape=jax.ShapeDtypeStruct((qcount, owned, 2, columns), jnp.float32),
        in_specs=[pl.BlockSpec(memory_space=pltpu.VMEM)] * 2,
        out_specs=pl.BlockSpec(memory_space=pltpu.VMEM),
        compiler_params=pltpu.CompilerParams(vmem_limit_bytes=24 * 2**20),
        name="factors",
    )(parts, factors)


def local(tau_slabs, lambda_slabs, aux_factor, transfer_table):
    groups = lax.axis_size("kring")
    virtuals = tau_slabs.shape[2]
    contracted = tau_slabs.shape[3]
    qcount = aux_factor.shape[0]
    rows = tau_slabs.shape[0] * 2 * virtuals
    owned = virtuals // groups
    packed, slots = pack(
        tau_slabs.reshape(rows, contracted), lambda_slabs.reshape(rows, contracted), transfer_table
    )
    packed = packed.reshape(groups, contracted // groups, 2 * rows)
    exchanged = lax.all_to_all(packed, "kring", 0, 0)
    partial = pair_terms(slots, exchanged, virtuals)
    near = ("kring", "y_lo", "z_lo")
    orb = ("y_lo", "z_hi", "z_lo")
    tiles = partial.reshape(lax.axis_size(near), SUBLANES, LANES)
    tile = lax.all_to_all(tiles, near, 0, 0).sum(0)
    copies = jnp.broadcast_to(tile[None], (lax.axis_size(orb),) + tile.shape)
    parts = lax.all_to_all(copies, orb, 0, 0)
    factors = aux_factor.reshape(qcount, 2 * virtuals, aux_factor.shape[3])
    gamma = factor_product(parts, factors, owned, lax.axis_size("z_hi"))
    return gamma.transpose(0, 2, 1, 3)


def solution(mesh):
    groups, spread = mesh.devices.shape
    parts = jax.sharding.Mesh(
        mesh.devices.reshape(groups, 2, spread // 4, 2), ("kring", "y_lo", "z_hi", "z_lo")
    )
    orb = ("y_lo", "z_hi", "z_lo")
    in_specs = (
        P("kring", None, None, orb),
        P("kring", None, None, orb),
        P(None, None, None, orb),
        P(),
    )
    out_specs = P(None, None, "kring", orb)
    return jax.shard_map(local, mesh=parts, in_specs=in_specs, out_specs=out_specs, check_vma=False)
```

time: 425 us -> 82.7 us (0.19)
  waiting for transfers between devices: 202 us -> 0 us
  matrix products: 50.5 us -> 0 us
  blocking collectives: 117 us -> 76.2 us
  starting transfers between devices: 35.7 us -> 0 us
  local copies, waits for them, and re-layouts: 15.5 us -> 0.02 us
  Pallas kernels: 0 us -> 5.81 us
    ppermute x15 -> x0, waiting for transfers between devices: 202 us -> none  [passed_along(): return lax.ppermute(value, axis, pairs)]
    psum x1 -> x0, blocking collectives: 117 us -> none  [local(): summed = lax.psum(totals, ('kring', 'orb'))]
    all_to_all x0 -> x3, blocking collectives: none -> 76.2 us  [the longest x1 34.2 us: local(): exchanged = lax.all_to_all(packed, 'kring', 0, 0)]
    dot_general x33 -> x0, matrix products: 50.5 us -> none  [the longest x16 28.9 us: pair_terms(): lax.dot_general(tau_rows, lambda_part, (((1,), (1,)), ((), ())), preferre...]
    ppermute x15 -> x0, starting transfers between devices: 35.7 us -> none  [passed_along(): return lax.ppermute(value, axis, pairs)]
    dynamic_slice x16 -> x0, local copies, waits for them, and re-layouts: 12.3 us -> none  [pair_terms(): lax.dynamic_slice(transfer_table, (anchor * triples, kring_index * triple...]
    pallas_call x0 -> x3, Pallas kernels: none -> 5.81 us  [the longest x1 2.75 us: pack(): pl.pallas_call(pack_kernel, out_shape=(jax.ShapeDtypeStruct((contracted,...]
  transfers between devices with their start and end apart: 15 -> 0, of which waited for: 15 -> 0; matrix products, arithmetic and copies ran while one was open for 3% -> 0% of each run, Pallas kernels for 0% -> 0%
where the time goes in v1:
time: 82.7 us; the launch traced here: 82.2 us
  blocking collectives  76.2 us (92%)
  Pallas kernels  5.81 us (7%)
    all_to_all x1, blocking collectives, local(): exchanged = lax.all_to_all(packed, 'kring', 0, 0)  34.2 us
    all_to_all x1, blocking collectives, local(): parts = lax.all_to_all(copies, orb, 0, 0)  28.3 us
    all_to_all x1, blocking collectives, local(): tile = lax.all_to_all(tiles, near, 0, 0).sum(0)  13.7 us
    pallas_call x1, Pallas kernels, pack(): pl.pallas_call(pack_kernel, out_shape=(jax.ShapeDtypeStruct((contracted,...  2.75 us
    pallas_call x1, Pallas kernels, pair_terms(): pl.pallas_call(lambda *refs: pair_kernel(virtuals, *refs), out_shape=jax....  1.99 us

profile of v1, /device:TPU:1, one launch (start us, length us, event | category | flops | bytes accessed | tf_op | source)
XLA Modules:
  0.0 82.2 jit_solution(13336184546312384408)
XLA Ops:
  0.0 2.8 %pack.1 = (bf16[896,896]{1,0:T(8,128)(2,1)}, s32[32,128]{1,0:T(8,128)}) custom-call(bf16[448,896]{1,0:T(8,128)(2,1)} %bitcast.9, bf16[448,896]{1,0:T(8,128)(2,1)} %bitcast.10, s32[32,32]{1,0:T(8,128)} %table_ref.1), custom_call_target="tpu_custom_call" | custom-call | tf_op jit(solution)/shard_map/pack/pallas_call | solution.py:68
  2.8 0.0 copy-start.1
  2.8 34.2 %all_to_all.15.refs_1_ = bf16[16,56,896]{2,1,0:T(8,128)(2,1)S(1)} all-to-all(bf16[16,56,896]{2,1,0:T(8,128)(2,1)} %bitcast.8), channel_id=1, replica_groups=mesh['kring'=16,'y_lo'=2,'z_hi'=8,'z_lo'=2] {'kring'}, dimensions={0} | all-to-all | bytes 3211264 | tf_op jit(solution)/shard_map/all_to_all | solution.py:221
  37.0 0.0 copy-start
  37.0 0.0 copy-done.1
  37.0 2.0 %pairs.1 = f32[16,32,128]{2,1,0:T(8,128)S(1)} custom-call(s32[32,128]{1,0:T(8,128)S(1)} %copy-done.1, bf16[16,56,896]{2,1,0:T(8,128)(2,1)S(1)} %all_to_all.15.refs_1_), custom_call_target="tpu_custom_call" | custom-call | tf_op jit(solution)/shard_map/pairs/pallas_call | solution.py:159
  39.0 13.7 %all_to_all.16 = f32[64,8,128]{2,1,0:T(8,128)S(1)} all-to-all(f32[64,8,128]{2,1,0:T(8,128)S(1)} %bitcast.7), channel_id=1, replica_groups=mesh['kring'=16,'y_lo'=2,'z_hi'=8,'z_lo'=2] {'kring','y_lo','z_lo'}, dimensions={0} | all-to-all | bytes 524288 | tf_op jit(solution)/shard_map/all_to_all | solution.py:226
  52.7 0.1 reduce_sum.9
  52.8 28.3 %all_to_all.17.refs_0_ = f32[32,8,128]{2,1,0:T(8,128)S(1)} all-to-all(f32[32,8,128]{2,1,0:T(8,128)S(1)} %broadcast_in_dim.2), channel_id=1, replica_groups=mesh['kring'=16,'y_lo'=2,'z_hi'=8,'z_lo'=2] {'y_lo','z_hi','z_lo'}, dimensions={0} | all-to-all | bytes 262144 | tf_op jit(solution)/shard_map/all_to_all | solution.py:228
  81.1 0.0 copy-done
  81.1 1.1 %factors.1 = f32[2,7,2,1680]{3,2,1,0:T(2,128)} custom-call(f32[32,8,128]{2,1,0:T(8,128)S(1)} %all_to_all.17.refs_0_, bf16[2,224,1680]{2,1,0:T(8,128)(2,1)S(1)} %bitcast.6), custom_call_target="tpu_custom_call" | custom-call | tf_op jit(solution)/shard_map/factors/pallas_call | solution.py:200
  (1 shorter events, 0.0 us)
Async XLA Ops:
  2.8 34.2 %copy-start.1 = (s32[32,128]{1,0:T(8,128)S(1)}, s32[32,128]{1,0:T(8,128)}, u32[]{:S(2)}) copy-start(s32[32,128]{1,0:T(8,128)} %get-tuple-element.7.refs_0_) | copy-start | bytes 49156
  37.0 44.1 %copy-start = (bf16[2,2,112,1680]{3,2,1,0:T(8,128)(2,1)S(1)}, bf16[2,2,112,1680]{3,2,1,0:T(8,128)(2,1)}, u32[]{:S(2)}) copy-start(bf16[2,2,112,1680]{3,2,1,0:T(8,128)(2,1)} %param.6) | copy-start | bytes 4515844

commit v2 on v1

--- a/solution.py
+++ b/solution.py
@@ -180,15 +180,19 @@
     for q in range(qcount):
         density = []
         for component in range(2):
-            total = parts_ref[q * far * 2 + component]
+            total = parts_ref[q * far * 2 + component].astype(jnp.float32)
             for step in range(1, far):
-                total += parts_ref[(q * far + step) * 2 + component]
-            density.append(total[:, :virtuals].astype(jnp.bfloat16).astype(jnp.float32))
+                total += parts_ref[(q * far + step) * 2 + component].astype(jnp.float32)
+            density.append(total[:, :virtuals])
         real, imag = density
         upper = jnp.concatenate([real, -imag], 1)
         lower = jnp.concatenate([imag, real], 1)
-        rows = jnp.concatenate([upper, lower], 0).astype(jnp.bfloat16)
-        gamma = jnp.dot(rows, factors_ref[q], preferred_element_type=jnp.float32)
+        rows = jnp.concatenate([upper, lower], 0)
+        high = rows.astype(jnp.bfloat16)
+        low = (rows - high.astype(jnp.float32)).astype(jnp.bfloat16)
+        both = jnp.concatenate([high, low], 0)
+        gamma = jnp.dot(both, factors_ref[q], preferred_element_type=jnp.float32)
+        gamma = gamma[: 2 * SUBLANES] + gamma[2 * SUBLANES :]
         for row in range(owned):
             out_ref[q, row] = jnp.concatenate(
                 [gamma[row : row + 1], gamma[SUBLANES + row : SUBLANES + row + 1]], 0
@@ -224,8 +228,11 @@
     orb = ("y_lo", "z_hi", "z_lo")
     tiles = partial.reshape(lax.axis_size(near), SUBLANES, LANES)
     tile = lax.all_to_all(tiles, near, 0, 0).sum(0)
+    tile = tile.astype(jnp.bfloat16)
     copies = jnp.broadcast_to(tile[None], (lax.axis_size(orb),) + tile.shape)
-    parts = lax.all_to_all(copies, orb, 0, 0)
+    half = lax.axis_size(orb) // 4
+    order = [[*range(half, 2 * half), *range(half), *range(2 * half, 4 * half)]]
+    parts = lax.all_to_all(copies, orb, 0, 0, axis_index_groups=order)
     factors = aux_factor.reshape(qcount, 2 * virtuals, aux_factor.shape[3])
     gamma = factor_product(parts, factors, owned, lax.axis_size("z_hi"))
     return gamma.transpose(0, 2, 1, 3)

time: 82.7 us -> 74.6 us (0.902)
  blocking collectives: 76.2 us -> 68.3 us
    all_to_all x1, blocking collectives: 28.3 us -> 20.4 us  [local(): parts = lax.all_to_all(copies, orb, 0, 0, axis_index_groups=order)]
where the time goes in v2:
time: 74.6 us; the launch traced here: 74.3 us
  blocking collectives  68.3 us (92%)
  Pallas kernels  5.87 us (8%)
    all_to_all x1, blocking collectives, local(): exchanged = lax.all_to_all(packed, 'kring', 0, 0)  34.2 us
    all_to_all x1, blocking collectives, local(): parts = lax.all_to_all(copies, orb, 0, 0, axis_index_groups=order)  20.4 us
    all_to_all x1, blocking collectives, local(): tile = lax.all_to_all(tiles, near, 0, 0).sum(0)  13.7 us
    pallas_call x1, Pallas kernels, pack(): pl.pallas_call(pack_kernel, out_shape=(jax.ShapeDtypeStruct((contracted,...  2.75 us
    pallas_call x1, Pallas kernels, pair_terms(): pl.pallas_call(lambda *refs: pair_kernel(virtuals, *refs), out_shape=jax....  1.99 us

profile of v2, /device:TPU:1, one launch (start us, length us, event | category | flops | bytes accessed | tf_op | source)
XLA Modules:
  0.0 74.3 jit_solution(10870559050238798053)
XLA Ops:
  0.0 2.8 %pack.1 = (bf16[896,896]{1,0:T(8,128)(2,1)}, s32[32,128]{1,0:T(8,128)}) custom-call(bf16[448,896]{1,0:T(8,128)(2,1)} %bitcast.9, bf16[448,896]{1,0:T(8,128)(2,1)} %bitcast.10, s32[32,32]{1,0:T(8,128)} %table_ref.1), custom_call_target="tpu_custom_call" | custom-call | tf_op jit(solution)/shard_map/pack/pallas_call | solution.py:68
  2.8 0.0 copy-start.1
  2.8 34.2 %all_to_all.15.refs_1_ = bf16[16,56,896]{2,1,0:T(8,128)(2,1)S(1)} all-to-all(bf16[16,56,896]{2,1,0:T(8,128)(2,1)} %bitcast.8), channel_id=1, replica_groups=mesh['kring'=16,'y_lo'=2,'z_hi'=8,'z_lo'=2] {'kring'}, dimensions={0} | all-to-all | bytes 3211264 | tf_op jit(solution)/shard_map/all_to_all | solution.py:225
  37.0 0.0 copy-start
  37.0 0.0 copy-done.1
  37.0 2.0 %pairs.1 = f32[16,32,128]{2,1,0:T(8,128)S(1)} custom-call(s32[32,128]{1,0:T(8,128)S(1)} %copy-done.1, bf16[16,56,896]{2,1,0:T(8,128)(2,1)S(1)} %all_to_all.15.refs_1_), custom_call_target="tpu_custom_call" | custom-call | tf_op jit(solution)/shard_map/pairs/pallas_call | solution.py:159
  39.0 13.7 %all_to_all.16 = f32[64,8,128]{2,1,0:T(8,128)S(1)} all-to-all(f32[64,8,128]{2,1,0:T(8,128)S(1)} %bitcast.7), channel_id=1, replica_groups=mesh['kring'=16,'y_lo'=2,'z_hi'=8,'z_lo'=2] {'kring','y_lo','z_lo'}, dimensions={0} | all-to-all | bytes 524288 | tf_op jit(solution)/shard_map/all_to_all | solution.py:230
  52.7 0.1 reduce_sum.9
  52.8 20.4 %all_to_all.17.refs_0_ = bf16[32,8,128]{2,1,0:T(8,128)(2,1)S(1)} all-to-all(bf16[32,8,128]{2,1,0:T(8,128)(2,1)S(1)} %broadcast_in_dim.2), channel_id=1, replica_groups={{8,9,10,11,12,13,14,15,0,1,2,3,4,5,6,7,16,17,18,19,20,21,22,23,24,25,26..., dimensions={0} | all-to-all | bytes 131072 | tf_op jit(solution)/shard_map/all_to_all | solution.py:235
  73.2 0.0 copy-done
  73.2 1.1 %factors.1 = f32[2,7,2,1680]{3,2,1,0:T(2,128)} custom-call(bf16[32,8,128]{2,1,0:T(8,128)(2,1)S(1)} %all_to_all.17.refs_0_, bf16[2,224,1680]{2,1,0:T(8,128)(2,1)S(1)} %bitcast.6), custom_call_target="tpu_custom_call" | custom-call | tf_op jit(solution)/shard_map/factors/pallas_call | solution.py:204
  (1 shorter events, 0.0 us)
Async XLA Ops:
  2.8 34.2 %copy-start.1 = (s32[32,128]{1,0:T(8,128)S(1)}, s32[32,128]{1,0:T(8,128)}, u32[]{:S(2)}) copy-start(s32[32,128]{1,0:T(8,128)} %get-tuple-element.7.refs_0_) | copy-start | bytes 49156
  37.0 36.2 %copy-start = (bf16[2,2,112,1680]{3,2,1,0:T(8,128)(2,1)S(1)}, bf16[2,2,112,1680]{3,2,1,0:T(8,128)(2,1)}, u32[]{:S(2)}) copy-start(bf16[2,2,112,1680]{3,2,1,0:T(8,128)(2,1)} %param.6) | copy-start | bytes 4515844

commit v3 on v2

--- a/solution.py
+++ b/solution.py
@@ -87,7 +87,7 @@
 
 
 def pair_kernel(
-    virtuals, slots_ref, packed_ref, out_ref, tau_part, lambda_part, chosen, slots, arrived
+    virtuals, ring, slots_ref, packed_ref, out_ref, tau_part, lambda_part, chosen, slots, arrived
 ):
     slots_copy = pltpu.make_async_copy(slots_ref, slots, arrived)
     slots_copy.start()
@@ -98,8 +98,8 @@
     half = width // 2
     fill = jnp.zeros((slot_rows - depth, half), jnp.float32)
     lane_fill = jnp.zeros((slot_rows, LANES - virtuals), jnp.bfloat16)
-    for group in range(groups):
-        block = packed_ref[group].astype(jnp.float32)
+    for place, group in enumerate(ring):
+        block = packed_ref[place].astype(jnp.float32)
         tau_block = jnp.concatenate([block[:, :half], fill], 0).astype(jnp.bfloat16)
         lambda_block = jnp.concatenate([block[:, half:], fill], 0).astype(jnp.bfloat16)
         for local_triple in range(2):
@@ -145,19 +145,20 @@
         imag_lambda = total[:, lane + LANES : lane + 2 * LANES]
         real_part = real_lambda[:virtuals] + imag_lambda[virtuals:]
         imag_part = real_lambda[virtuals:] - imag_lambda[:virtuals]
-        for place, part in ((2 * q, real_part), (2 * q + 1, imag_part)):
-            for group in range(groups):
-                out_ref[group, place * SUBLANES : (place + 1) * SUBLANES] = jnp.concatenate(
+        for component, part in enumerate((real_part, imag_part)):
+            row = (2 * q + component) * SUBLANES
+            for place, group in enumerate(ring):
+                out_ref[place, row : row + SUBLANES] = jnp.concatenate(
                     [part[group * owned : (group + 1) * owned], blank], 0
                 )
 
 
-def pair_terms(slots, packed, virtuals):
+def pair_terms(slots, packed, virtuals, ring):
     groups, depth, width = packed.shape
     slot_rows = -(-depth // 16) * 16
     triples = 2 * groups
     return pl.pallas_call(
-        lambda *refs: pair_kernel(virtuals, *refs),
+        lambda *refs: pair_kernel(virtuals, ring, *refs),
         out_shape=jax.ShapeDtypeStruct((groups, 4 * SUBLANES, LANES), jnp.float32),
         in_specs=[pl.BlockSpec(memory_space=pl.ANY), pl.BlockSpec(memory_space=pltpu.VMEM)],
         out_specs=pl.BlockSpec(memory_space=pltpu.VMEM),
@@ -222,12 +223,16 @@
         tau_slabs.reshape(rows, contracted), lambda_slabs.reshape(rows, contracted), transfer_table
     )
     packed = packed.reshape(groups, contracted // groups, 2 * rows)
-    exchanged = lax.all_to_all(packed, "kring", 0, 0)
-    partial = pair_terms(slots, exchanged, virtuals)
+    start = groups - groups // 4
+    ring = [*range(start, groups), *range(start)]
+    exchanged = lax.all_to_all(packed, "kring", 0, 0, axis_index_groups=[ring])
+    partial = pair_terms(slots, exchanged, virtuals, ring)
     near = ("kring", "y_lo", "z_lo")
     orb = ("y_lo", "z_hi", "z_lo")
+    pieces = lax.axis_size(near) // groups
+    members = [[group * pieces + piece for group in ring for piece in range(pieces)]]
     tiles = partial.reshape(lax.axis_size(near), SUBLANES, LANES)
-    tile = lax.all_to_all(tiles, near, 0, 0).sum(0)
+    tile = lax.all_to_all(tiles, near, 0, 0, axis_index_groups=members).sum(0)
     tile = tile.astype(jnp.bfloat16)
     copies = jnp.broadcast_to(tile[None], (lax.axis_size(orb),) + tile.shape)
     half = lax.axis_size(orb) // 4

time: 74.6 us -> 72.1 us (0.966)
  blocking collectives: 68.3 us -> 65.7 us
    all_to_all x2, blocking collectives: 48 us -> 46.4 us  [the longest x1 32.6 us: local(): exchanged = lax.all_to_all(packed, 'kring', 0, 0, axis_index_groups=[ring])]
    all_to_all x1, blocking collectives: 20.4 us -> 19.2 us  [local(): parts = lax.all_to_all(copies, orb, 0, 0, axis_index_groups=order)]
where the time goes in v3:
time: 72.1 us; the launch traced here: 71.7 us
  blocking collectives  65.7 us (91%)
  Pallas kernels  5.87 us (8%)
    all_to_all x1, blocking collectives, local(): exchanged = lax.all_to_all(packed, 'kring', 0, 0, axis_index_groups=[ring])  32.6 us
    all_to_all x1, blocking collectives, local(): parts = lax.all_to_all(copies, orb, 0, 0, axis_index_groups=order)  19.2 us
    all_to_all x1, blocking collectives, local(): tile = lax.all_to_all(tiles, near, 0, 0, axis_index_groups=members).sum(0)  13.9 us
    pallas_call x1, Pallas kernels, pack(): pl.pallas_call(pack_kernel, out_shape=(jax.ShapeDtypeStruct((contracted,...  2.75 us
    pallas_call x1, Pallas kernels, pair_terms(): pl.pallas_call(lambda *refs: pair_kernel(virtuals, ring, *refs), out_shap...  1.99 us

profile of v3, /device:TPU:1, one launch (start us, length us, event | category | flops | bytes accessed | tf_op | source)
XLA Modules:
  0.0 71.7 jit_solution(17135574868439781932)
XLA Ops:
  0.0 2.8 %pack.1 = (bf16[896,896]{1,0:T(8,128)(2,1)}, s32[32,128]{1,0:T(8,128)}) custom-call(bf16[448,896]{1,0:T(8,128)(2,1)} %bitcast.9, bf16[448,896]{1,0:T(8,128)(2,1)} %bitcast.10, s32[32,32]{1,0:T(8,128)} %table_ref.1), custom_call_target="tpu_custom_call" | custom-call | tf_op jit(solution)/shard_map/pack/pallas_call | solution.py:68
  2.8 0.0 copy-start.1
  2.8 32.6 %all_to_all.15.refs_1_ = bf16[16,56,896]{2,1,0:T(8,128)(2,1)S(1)} all-to-all(bf16[16,56,896]{2,1,0:T(8,128)(2,1)} %bitcast.8), channel_id=1, replica_groups={{384,416,448,480,0,32,64,96,128,160,192,224,256,288,320,352},{385,417,4..., dimensions={0} | all-to-all | bytes 3211264 | tf_op jit(solution)/shard_map/all_to_all | solution.py:228
  35.3 0.0 copy-start
  35.3 0.0 copy-done.1
  35.4 2.0 %pairs.1 = f32[16,32,128]{2,1,0:T(8,128)S(1)} custom-call(s32[32,128]{1,0:T(8,128)S(1)} %copy-done.1, bf16[16,56,896]{2,1,0:T(8,128)(2,1)S(1)} %all_to_all.15.refs_1_), custom_call_target="tpu_custom_call" | custom-call | tf_op jit(solution)/shard_map/pairs/pallas_call | solution.py:160
  37.3 13.9 %all_to_all.16 = f32[64,8,128]{2,1,0:T(8,128)S(1)} all-to-all(f32[64,8,128]{2,1,0:T(8,128)S(1)} %bitcast.7), channel_id=1, replica_groups={{384,385,400,401,416,417,432,433,448,449,464,465,480,481,496,497,0,1,16..., dimensions={0} | all-to-all | bytes 524288 | tf_op jit(solution)/shard_map/all_to_all | solution.py:235
  51.2 0.1 reduce_sum.9
  51.3 19.2 %all_to_all.17.refs_0_ = bf16[32,8,128]{2,1,0:T(8,128)(2,1)S(1)} all-to-all(bf16[32,8,128]{2,1,0:T(8,128)(2,1)S(1)} %broadcast_in_dim.2), channel_id=1, replica_groups={{8,9,10,11,12,13,14,15,0,1,2,3,4,5,6,7,16,17,18,19,20,21,22,23,24,25,26..., dimensions={0} | all-to-all | bytes 131072 | tf_op jit(solution)/shard_map/all_to_all | solution.py:240
  70.5 0.0 copy-done
  70.5 1.1 %factors.1 = f32[2,7,2,1680]{3,2,1,0:T(2,128)} custom-call(bf16[32,8,128]{2,1,0:T(8,128)(2,1)S(1)} %all_to_all.17.refs_0_, bf16[2,224,1680]{2,1,0:T(8,128)(2,1)S(1)} %bitcast.6), custom_call_target="tpu_custom_call" | custom-call | tf_op jit(solution)/shard_map/factors/pallas_call | solution.py:205
  (1 shorter events, 0.0 us)
Async XLA Ops:
  2.8 32.6 %copy-start.1 = (s32[32,128]{1,0:T(8,128)S(1)}, s32[32,128]{1,0:T(8,128)}, u32[]{:S(2)}) copy-start(s32[32,128]{1,0:T(8,128)} %get-tuple-element.7.refs_0_) | copy-start | bytes 49156
  35.3 35.2 %copy-start = (bf16[2,2,112,1680]{3,2,1,0:T(8,128)(2,1)S(1)}, bf16[2,2,112,1680]{3,2,1,0:T(8,128)(2,1)}, u32[]{:S(2)}) copy-start(bf16[2,2,112,1680]{3,2,1,0:T(8,128)(2,1)} %param.6) | copy-start | bytes 4515844

commit v4 on v3

--- a/solution.py
+++ b/solution.py
@@ -25,23 +25,25 @@
 
 
 def pack_kernel(
-    tau_ref, lambda_ref, table_ref, packed_ref, slots_ref, both, turned, table_here, slots_here, arrived, left
+    virtuals, tau_ref, lambda_ref, table_ref, packed_ref, slots_ref, both, turned, table_here,
+    slots_here, arrived, left
 ):
-    rows, contracted = tau_ref.shape
-    tiles = contracted // LANES
-    table_copy = pltpu.make_async_copy(table_ref, table_here, arrived.at[2 * tiles])
+    contracted = both.shape[1]
+    tiles = both.shape[0] // LANES
+    spare = LANES - virtuals
+    whole = [(lambda_ref, at) for at in range(4)] + [(tau_ref, at) for at in range(3)]
+    moves = [(source, at * virtuals, tile * LANES, virtuals) for tile, (source, at) in enumerate(whole)]
+    for tile in range(tiles):
+        moves.append((tau_ref, 3 * virtuals + tile * spare, tile * LANES + virtuals, spare))
+    incoming = []
+    for number, (source, start, place, size) in enumerate(moves):
+        incoming.append(
+            pltpu.make_async_copy(
+                source.at[pl.ds(start, size)], both.at[pl.ds(place, size)], arrived.at[number]
+            )
+        )
+    table_copy = pltpu.make_async_copy(table_ref, table_here, arrived.at[len(moves)])
     table_copy.start()
-    incoming = []
-    for tile in range(tiles):
-        lanes = pl.ds(tile * LANES, LANES)
-        for part, source in enumerate((tau_ref, lambda_ref)):
-            incoming.append(
-                pltpu.make_async_copy(
-                    source.at[:, lanes],
-                    both.at[tile, pl.ds(part * rows, rows)],
-                    arrived.at[2 * tile + part],
-                )
-            )
     for copy in incoming:
         copy.start()
     table_copy.wait()
@@ -49,12 +51,13 @@
     slots_copy = pltpu.make_async_copy(slots_here, slots_ref, left.at[tiles])
     slots_copy.start()
     outgoing = [slots_copy]
-    for tile in range(tiles):
-        incoming[2 * tile].wait()
-        incoming[2 * tile + 1].wait()
-        turned[tile] = both[tile].T
+    for copy in incoming:
+        copy.wait()
+    for tile in range(contracted // LANES):
+        start = tile * LANES
+        turned[start : start + LANES] = both[:, start : start + LANES].T
         copy = pltpu.make_async_copy(
-            turned.at[tile], packed_ref.at[pl.ds(tile * LANES, LANES)], left.at[tile]
+            turned.at[pl.ds(start, LANES)], packed_ref.at[pl.ds(start, LANES)], left.at[tile]
         )
         copy.start()
         outgoing.append(copy)
@@ -62,11 +65,11 @@
         copy.wait()
 
 
-def pack(tau_rows, lambda_rows, table):
+def pack(tau_rows, lambda_rows, table, virtuals):
     rows, contracted = tau_rows.shape
-    tiles = contracted // LANES
+    tiles = 2 * rows // LANES
     return pl.pallas_call(
-        pack_kernel,
+        lambda *refs: pack_kernel(virtuals, *refs),
         out_shape=(
             jax.ShapeDtypeStruct((contracted, 2 * rows), jnp.bfloat16),
             jax.ShapeDtypeStruct((table.shape[0], LANES), jnp.int32),
@@ -74,8 +77,8 @@
         in_specs=[pl.BlockSpec(memory_space=pltpu.HBM)] * 3,
         out_specs=(pl.BlockSpec(memory_space=pltpu.HBM),) * 2,
         scratch_shapes=[
-            pltpu.VMEM((tiles, 2 * rows, LANES), jnp.bfloat16),
-            pltpu.VMEM((tiles, LANES, 2 * rows), jnp.bfloat16),
+            pltpu.VMEM((2 * rows, contracted), jnp.bfloat16),
+            pltpu.VMEM((contracted, 2 * rows), jnp.bfloat16),
             pltpu.VMEM(table.shape, jnp.int32),
             pltpu.VMEM((table.shape[0], LANES), jnp.int32),
             pltpu.SemaphoreType.DMA((2 * tiles + 1,)),
@@ -87,7 +90,7 @@
 
 
 def pair_kernel(
-    virtuals, ring, slots_ref, packed_ref, out_ref, tau_part, lambda_part, chosen, slots, arrived
+    virtuals, ring, slots_ref, packed_ref, out_ref, tau_part, chosen, slots, arrived
 ):
     slots_copy = pltpu.make_async_copy(slots_ref, slots, arrived)
     slots_copy.start()
@@ -95,56 +98,53 @@
     triples = 2 * groups
     slot_rows = tau_part.shape[1]
     qcount = 2
-    half = width // 2
-    fill = jnp.zeros((slot_rows - depth, half), jnp.float32)
-    lane_fill = jnp.zeros((slot_rows, LANES - virtuals), jnp.bfloat16)
+    pair = 2 * LANES
+    spare = LANES - virtuals
+    fill = jnp.zeros((slot_rows - depth, pair), jnp.bfloat16)
+
+    def deep(value):
+        return jnp.concatenate([value, fill], 0)
+
     for place, group in enumerate(ring):
-        block = packed_ref[place].astype(jnp.float32)
-        tau_block = jnp.concatenate([block[:, :half], fill], 0).astype(jnp.bfloat16)
-        lambda_block = jnp.concatenate([block[:, half:], fill], 0).astype(jnp.bfloat16)
-        for local_triple in range(2):
-            start = local_triple * 2 * virtuals
-            tau_part[2 * group + local_triple] = tau_block[:, start : start + 2 * virtuals]
-            lambda_part[2 * group + local_triple] = jnp.concatenate(
-                [
-                    lambda_block[:, start : start + virtuals],
-                    lane_fill,
-                    lambda_block[:, start + virtuals : start + 2 * virtuals],
-                    lane_fill,
-                ],
-                1,
+        tau_part[2 * group] = deep(packed_ref[place, :, 2 * pair : 3 * pair])
+        scattered = [
+            packed_ref[place, :, tile * LANES + virtuals : (tile + 1) * LANES]
+            for tile in range(width // LANES)
+        ]
+        last = packed_ref[place, :, 3 * pair : 3 * pair + LANES]
+        unused = jnp.zeros((depth, spare), jnp.bfloat16)
+        tau_part[2 * group + 1] = deep(jnp.concatenate([last] + scattered + [unused], 1))
+    slots_copy.wait()
+    for triple in range(triples):
+        for slot in range(2):
+            partner = slots[triple, slot]
+            transfer = slots[triple, 2 + slot]
+            place = lax.rem(partner // 2 + groups - ring[0], groups)
+            value = jnp.where(
+                partner % 2 == 0, packed_ref[place, :, :pair], packed_ref[place, :, pair : 2 * pair]
             )
-
-    slots_copy.wait()
-
-    def choose(slot, triple):
-        value = lambda_part[slots[triple, slot]]
-        transfer = slots[triple, 2 + slot]
-        for q in range(qcount):
-            chosen[slot, triple, :, q * 2 * LANES : (q + 1) * 2 * LANES] = jnp.where(
-                transfer == q, value, jnp.zeros_like(value)
-            )
-
-    for triple in range(triples):
-        choose(0, triple)
-        choose(1, triple)
-    tau_all = tau_part[...].reshape(triples * slot_rows, 2 * virtuals)
-    total = jnp.zeros((2 * virtuals, qcount * 2 * LANES), jnp.float32)
-    for slot in range(2):
-        total += lax.dot_general(
-            tau_all,
-            chosen[slot].reshape(triples * slot_rows, qcount * 2 * LANES),
-            (((0,), (0,)), ((), ())),
-            preferred_element_type=jnp.float32,
-        )
+            value = deep(value)
+            for q in range(qcount):
+                lane = (slot * qcount + q) * pair
+                chosen[triple, :, lane : lane + pair] = jnp.where(
+                    transfer == q, value, jnp.zeros_like(value)
+                )
+    wide = qcount * pair
+    products = lax.dot_general(
+        tau_part[...].reshape(triples * slot_rows, pair),
+        chosen[...].reshape(triples * slot_rows, 2 * wide),
+        (((0,), (0,)), ((), ())),
+        preferred_element_type=jnp.float32,
+    )
+    total = products[:, :wide] + products[:, wide:]
     owned = virtuals // groups
     blank = jnp.zeros((SUBLANES - owned, LANES), jnp.float32)
     for q in range(qcount):
         lane = q * 2 * LANES
         real_lambda = total[:, lane : lane + LANES]
         imag_lambda = total[:, lane + LANES : lane + 2 * LANES]
-        real_part = real_lambda[:virtuals] + imag_lambda[virtuals:]
-        imag_part = real_lambda[virtuals:] - imag_lambda[:virtuals]
+        real_part = real_lambda[:LANES] + imag_lambda[LANES:]
+        imag_part = real_lambda[LANES:] - imag_lambda[:LANES]
         for component, part in enumerate((real_part, imag_part)):
             row = (2 * q + component) * SUBLANES
             for place, group in enumerate(ring):
@@ -163,9 +163,8 @@
         in_specs=[pl.BlockSpec(memory_space=pl.ANY), pl.BlockSpec(memory_space=pltpu.VMEM)],
         out_specs=pl.BlockSpec(memory_space=pltpu.VMEM),
         scratch_shapes=[
-            pltpu.VMEM((triples, slot_rows, 2 * virtuals), jnp.bfloat16),
             pltpu.VMEM((triples, slot_rows, 2 * LANES), jnp.bfloat16),
-            pltpu.VMEM((2, triples, slot_rows, 4 * LANES), jnp.bfloat16),
+            pltpu.VMEM((triples, slot_rows, 8 * LANES), jnp.bfloat16),
             pltpu.SMEM(slots.shape, jnp.int32),
             pltpu.SemaphoreType.DMA,
         ],
@@ -220,7 +219,7 @@
     rows = tau_slabs.shape[0] * 2 * virtuals
     owned = virtuals // groups
     packed, slots = pack(
-        tau_slabs.reshape(rows, contracted), lambda_slabs.reshape(rows, contracted), transfer_table
+        tau_slabs.reshape(rows, contracted), lambda_slabs.reshape(rows, contracted), transfer_table, virtuals
     )
     packed = packed.reshape(groups, contracted // groups, 2 * rows)
     start = groups - groups // 4

time: 72.1 us -> 72.4 us (level)
  no operation moved by 1% of the time
where the time goes in v4:
time: 72.4 us; the launch traced here: 72 us
  blocking collectives  65.7 us (91%)
  Pallas kernels  6.19 us (9%)
    all_to_all x1, blocking collectives, local(): exchanged = lax.all_to_all(packed, 'kring', 0, 0, axis_index_groups=[ring])  32.6 us
    all_to_all x1, blocking collectives, local(): parts = lax.all_to_all(copies, orb, 0, 0, axis_index_groups=order)  19.2 us
    all_to_all x1, blocking collectives, local(): tile = lax.all_to_all(tiles, near, 0, 0, axis_index_groups=members).sum(0)  13.9 us
    pallas_call x1, Pallas kernels, pack(): pl.pallas_call(lambda *refs: pack_kernel(virtuals, *refs), out_shape=(jax...  2.91 us
    pallas_call x1, Pallas kernels, pair_terms(): pl.pallas_call(lambda *refs: pair_kernel(virtuals, ring, *refs), out_shap...  2.15 us

profile of v4, /device:TPU:1, one launch (start us, length us, event | category | flops | bytes accessed | tf_op | source)
XLA Modules:
  0.0 72.0 jit_solution(13203340217590538901)
XLA Ops:
  0.0 2.9 %pack.1 = (bf16[896,896]{1,0:T(8,128)(2,1)}, s32[32,128]{1,0:T(8,128)}) custom-call(bf16[448,896]{1,0:T(8,128)(2,1)} %bitcast.9, bf16[448,896]{1,0:T(8,128)(2,1)} %bitcast.10, s32[32,32]{1,0:T(8,128)} %refs_2_.1), custom_call_target="tpu_custom_call" | custom-call | tf_op jit(solution)/shard_map/pack/pallas_call | solution.py:71
  2.9 0.0 copy-start.1
  2.9 32.6 %all_to_all.15.refs_1_ = bf16[16,56,896]{2,1,0:T(8,128)(2,1)S(1)} all-to-all(bf16[16,56,896]{2,1,0:T(8,128)(2,1)} %bitcast.8), channel_id=1, replica_groups={{384,416,448,480,0,32,64,96,128,160,192,224,256,288,320,352},{385,417,4..., dimensions={0} | all-to-all | bytes 3211264 | tf_op jit(solution)/shard_map/all_to_all | solution.py:227
  35.5 0.0 copy-start
  35.5 0.0 copy-done.1
  35.5 2.1 %pairs.1 = f32[16,32,128]{2,1,0:T(8,128)S(1)} custom-call(s32[32,128]{1,0:T(8,128)S(1)} %copy-done.1, bf16[16,56,896]{2,1,0:T(8,128)(2,1)S(1)} %all_to_all.15.refs_1_), custom_call_target="tpu_custom_call" | custom-call | tf_op jit(solution)/shard_map/pairs/pallas_call | solution.py:160
  37.7 13.9 %all_to_all.16 = f32[64,8,128]{2,1,0:T(8,128)S(1)} all-to-all(f32[64,8,128]{2,1,0:T(8,128)S(1)} %bitcast.7), channel_id=1, replica_groups={{384,385,400,401,416,417,432,433,448,449,464,465,480,481,496,497,0,1,16..., dimensions={0} | all-to-all | bytes 524288 | tf_op jit(solution)/shard_map/all_to_all | solution.py:234
  51.5 0.1 reduce_sum.9
  51.6 19.2 %all_to_all.17.refs_0_ = bf16[32,8,128]{2,1,0:T(8,128)(2,1)S(1)} all-to-all(bf16[32,8,128]{2,1,0:T(8,128)(2,1)S(1)} %broadcast_in_dim.2), channel_id=1, replica_groups={{8,9,10,11,12,13,14,15,0,1,2,3,4,5,6,7,16,17,18,19,20,21,22,23,24,25,26..., dimensions={0} | all-to-all | bytes 131072 | tf_op jit(solution)/shard_map/all_to_all | solution.py:239
  70.8 0.0 copy-done
  70.8 1.1 %factors.1 = f32[2,7,2,1680]{3,2,1,0:T(2,128)} custom-call(bf16[32,8,128]{2,1,0:T(8,128)(2,1)S(1)} %all_to_all.17.refs_0_, bf16[2,224,1680]{2,1,0:T(8,128)(2,1)S(1)} %bitcast.6), custom_call_target="tpu_custom_call" | custom-call | tf_op jit(solution)/shard_map/factors/pallas_call | solution.py:204
  (1 shorter events, 0.0 us)
Async XLA Ops:
  2.9 32.6 %copy-start.1 = (s32[32,128]{1,0:T(8,128)S(1)}, s32[32,128]{1,0:T(8,128)}, u32[]{:S(2)}) copy-start(s32[32,128]{1,0:T(8,128)} %get-tuple-element.7.refs_0_) | copy-start | bytes 49156
  35.5 35.3 %copy-start = (bf16[2,2,112,1680]{3,2,1,0:T(8,128)(2,1)S(1)}, bf16[2,2,112,1680]{3,2,1,0:T(8,128)(2,1)}, u32[]{:S(2)}) copy-start(bf16[2,2,112,1680]{3,2,1,0:T(8,128)(2,1)} %param.6) | copy-start | bytes 4515844

commit v5 on v3

--- a/solution.py
+++ b/solution.py
@@ -7,6 +7,8 @@
 
 LANES = 128
 SUBLANES = 8
+SMALLEST = 2.0**-100
+HEADROOM = 13.0
 
 
 def partner_slots(table, shape):
@@ -121,7 +123,8 @@
         value = lambda_part[slots[triple, slot]]
         transfer = slots[triple, 2 + slot]
         for q in range(qcount):
-            chosen[slot, triple, :, q * 2 * LANES : (q + 1) * 2 * LANES] = jnp.where(
+            lane = (slot * qcount + q) * 2 * LANES
+            chosen[triple, :, lane : lane + 2 * LANES] = jnp.where(
                 transfer == q, value, jnp.zeros_like(value)
             )
 
@@ -129,28 +132,35 @@
         choose(0, triple)
         choose(1, triple)
     tau_all = tau_part[...].reshape(triples * slot_rows, 2 * virtuals)
-    total = jnp.zeros((2 * virtuals, qcount * 2 * LANES), jnp.float32)
-    for slot in range(2):
-        total += lax.dot_general(
-            tau_all,
-            chosen[slot].reshape(triples * slot_rows, qcount * 2 * LANES),
-            (((0,), (0,)), ((), ())),
-            preferred_element_type=jnp.float32,
-        )
+    wide = qcount * 2 * LANES
+    products = lax.dot_general(
+        tau_all,
+        chosen[...].reshape(triples * slot_rows, 2 * wide),
+        (((0,), (0,)), ((), ())),
+        preferred_element_type=jnp.float32,
+    )
+    total = products[:, :wide] + products[:, wide:]
     owned = virtuals // groups
-    blank = jnp.zeros((SUBLANES - owned, LANES), jnp.float32)
+    pieces = []
     for q in range(qcount):
         lane = q * 2 * LANES
         real_lambda = total[:, lane : lane + LANES]
         imag_lambda = total[:, lane + LANES : lane + 2 * LANES]
-        real_part = real_lambda[:virtuals] + imag_lambda[virtuals:]
-        imag_part = real_lambda[virtuals:] - imag_lambda[:virtuals]
-        for component, part in enumerate((real_part, imag_part)):
-            row = (2 * q + component) * SUBLANES
-            for place, group in enumerate(ring):
-                out_ref[place, row : row + SUBLANES] = jnp.concatenate(
-                    [part[group * owned : (group + 1) * owned], blank], 0
-                )
+        pieces.append(real_lambda[:virtuals] + imag_lambda[virtuals:])
+        pieces.append(real_lambda[virtuals:] - imag_lambda[:virtuals])
+    largest = jnp.abs(pieces[0])
+    for piece in pieces[1:]:
+        largest = jnp.maximum(largest, jnp.abs(piece))
+    largest = jnp.max(jnp.max(largest, 0, keepdims=True), 1, keepdims=True)
+    exponent = jnp.floor(jnp.log2(jnp.maximum(largest, SMALLEST)))
+    scale = jnp.exp2(HEADROOM - exponent)
+    note = jnp.broadcast_to(exponent, (SUBLANES - owned, LANES))
+    for number, piece in enumerate(pieces):
+        scaled = piece * scale
+        for place, group in enumerate(ring):
+            out_ref[place, number * SUBLANES : (number + 1) * SUBLANES] = jnp.concatenate(
+                [scaled[group * owned : (group + 1) * owned], note], 0
+            ).astype(out_ref.dtype)
 
 
 def pair_terms(slots, packed, virtuals, ring):
@@ -165,7 +175,7 @@
         scratch_shapes=[
             pltpu.VMEM((triples, slot_rows, 2 * virtuals), jnp.bfloat16),
             pltpu.VMEM((triples, slot_rows, 2 * LANES), jnp.bfloat16),
-            pltpu.VMEM((2, triples, slot_rows, 4 * LANES), jnp.bfloat16),
+            pltpu.VMEM((triples, slot_rows, 8 * LANES), jnp.bfloat16),
             pltpu.SMEM(slots.shape, jnp.int32),
             pltpu.SemaphoreType.DMA,
         ],
@@ -224,15 +234,16 @@
     )
     packed = packed.reshape(groups, contracted // groups, 2 * rows)
     start = groups - groups // 4
-    ring = [*range(start, groups), *range(start)]
+    ring = [group ^ 1 for group in [*range(start, groups), *range(start)]]
     exchanged = lax.all_to_all(packed, "kring", 0, 0, axis_index_groups=[ring])
     partial = pair_terms(slots, exchanged, virtuals, ring)
     near = ("kring", "y_lo", "z_lo")
     orb = ("y_lo", "z_hi", "z_lo")
     pieces = lax.axis_size(near) // groups
     members = [[group * pieces + piece for group in ring for piece in range(pieces)]]
-    tiles = partial.reshape(lax.axis_size(near), SUBLANES, LANES)
-    tile = lax.all_to_all(tiles, near, 0, 0, axis_index_groups=members).sum(0)
+    tiles = partial.reshape(lax.axis_size(near), SUBLANES, LANES).astype(jnp.float16)
+    tiles = lax.all_to_all(tiles, near, 0, 0, axis_index_groups=members).astype(jnp.float32)
+    tile = (tiles * jnp.exp2(tiles[:, owned : owned + 1, :] - HEADROOM)).sum(0)
     tile = tile.astype(jnp.bfloat16)
     copies = jnp.broadcast_to(tile[None], (lax.axis_size(orb),) + tile.shape)
     half = lax.axis_size(orb) // 4

time: 72.1 us -> 70.1 us (0.972)
  blocking collectives: 65.7 us -> 63.4 us
    all_to_all x1, blocking collectives: 13.9 us -> 12 us  [local(): lax.all_to_all(tiles, near, 0, 0, axis_index_groups=members)]
where the time goes in v5:
time: 70.1 us; the launch traced here: 69.7 us
  blocking collectives  63.4 us (90%)
  Pallas kernels  6.01 us (9%)
    all_to_all x1, blocking collectives, local(): exchanged = lax.all_to_all(packed, 'kring', 0, 0, axis_index_groups=[ring])  32.3 us
    all_to_all x1, blocking collectives, local(): parts = lax.all_to_all(copies, orb, 0, 0, axis_index_groups=order)  19.2 us
    all_to_all x1, blocking collectives, local(): lax.all_to_all(tiles, near, 0, 0, axis_index_groups=members)  12 us
    pallas_call x1, Pallas kernels, pack(): pl.pallas_call(pack_kernel, out_shape=(jax.ShapeDtypeStruct((contracted,...  2.75 us
    pallas_call x1, Pallas kernels, pair_terms(): pl.pallas_call(lambda *refs: pair_kernel(virtuals, ring, *refs), out_shap...  2.13 us

profile of v5, /device:TPU:1, one launch (start us, length us, event | category | flops | bytes accessed | tf_op | source)
XLA Modules:
  0.0 69.7 jit_solution(14945304448168807099)
XLA Ops:
  0.0 2.8 %pack.1 = (bf16[896,896]{1,0:T(8,128)(2,1)}, s32[32,128]{1,0:T(8,128)}) custom-call(bf16[448,896]{1,0:T(8,128)(2,1)} %bitcast.9, bf16[448,896]{1,0:T(8,128)(2,1)} %bitcast.10, s32[32,32]{1,0:T(8,128)} %table_ref.1), custom_call_target="tpu_custom_call" | custom-call | tf_op jit(solution)/shard_map/pack/pallas_call | solution.py:70
  2.8 0.0 copy-start.1
  2.8 32.3 %all_to_all.15.refs_1_ = bf16[16,56,896]{2,1,0:T(8,128)(2,1)S(1)} all-to-all(bf16[16,56,896]{2,1,0:T(8,128)(2,1)} %bitcast.8), channel_id=1, replica_groups={{416,384,480,448,32,0,96,64,160,128,224,192,288,256,352,320},{417,385,4..., dimensions={0} | all-to-all | bytes 3211264 | tf_op jit(solution)/shard_map/all_to_all | solution.py:238
  35.0 0.0 copy-done.1
  35.0 0.0 copy-start
  35.0 2.1 %pairs.1 = f32[16,32,128]{2,1,0:T(8,128)S(1)} custom-call(s32[32,128]{1,0:T(8,128)S(1)} %copy-done.1, bf16[16,56,896]{2,1,0:T(8,128)(2,1)S(1)} %all_to_all.15.refs_1_), custom_call_target="tpu_custom_call" | custom-call | tf_op jit(solution)/shard_map/pairs/pallas_call | solution.py:170
  37.2 12.0 %all_to_all.16 = f16[64,8,128]{2,1,0:T(8,128)(2,1)S(1)} all-to-all(f16[64,8,128]{2,1,0:T(8,128)(2,1)S(1)} %bitcast.11), channel_id=1, replica_groups={{416,417,432,433,384,385,400,401,480,481,496,497,448,449,464,465,32,33,..., dimensions={0} | all-to-all | bytes 262144 | tf_op jit(solution)/shard_map/all_to_all | solution.py:245
  49.2 0.1 fusion.1
  49.3 0.1 multiply_reduce_fusion
  49.4 19.2 %all_to_all.17.refs_0_ = bf16[32,8,128]{2,1,0:T(8,128)(2,1)S(1)} all-to-all(bf16[32,8,128]{2,1,0:T(8,128)(2,1)S(1)} %broadcast_in_dim.2), channel_id=1, replica_groups={{8,9,10,11,12,13,14,15,0,1,2,3,4,5,6,7,16,17,18,19,20,21,22,23,24,25,26..., dimensions={0} | all-to-all | bytes 131072 | tf_op jit(solution)/shard_map/all_to_all | solution.py:251
  68.5 0.0 copy-done
  68.5 1.1 %factors.1 = f32[2,7,2,1680]{3,2,1,0:T(2,128)} custom-call(bf16[32,8,128]{2,1,0:T(8,128)(2,1)S(1)} %all_to_all.17.refs_0_, bf16[2,224,1680]{2,1,0:T(8,128)(2,1)S(1)} %bitcast.7), custom_call_target="tpu_custom_call" | custom-call | tf_op jit(solution)/shard_map/factors/pallas_call | solution.py:215
  (3 shorter events, 0.1 us)
Async XLA Ops:
  2.8 32.3 %copy-start.1 = (s32[32,128]{1,0:T(8,128)S(1)}, s32[32,128]{1,0:T(8,128)}, u32[]{:S(2)}) copy-start(s32[32,128]{1,0:T(8,128)} %get-tuple-element.7.refs_0_) | copy-start | bytes 49156
  35.0 33.5 %copy-start = (bf16[2,2,112,1680]{3,2,1,0:T(8,128)(2,1)S(1)}, bf16[2,2,112,1680]{3,2,1,0:T(8,128)(2,1)}, u32[]{:S(2)}) copy-start(bf16[2,2,112,1680]{3,2,1,0:T(8,128)(2,1)} %param.6) | copy-start | bytes 4515844

commit v6 on v5

--- a/solution.py
+++ b/solution.py
@@ -9,6 +9,7 @@
 SUBLANES = 8
 SMALLEST = 2.0**-100
 HEADROOM = 13.0
+SUM_HEADROOM = 7.0
 
 
 def partner_slots(table, shape):
@@ -184,39 +185,48 @@
     )(slots, packed)
 
 
-def factor_kernel(far, parts_ref, factors_ref, out_ref):
+def factor_kernel(far, parts_ref, factors_ref, out_ref, held, left):
     qcount, depth, _ = factors_ref.shape
     owned = out_ref.shape[1]
     virtuals = depth // 2
+
+    def unscaled(at):
+        part = parts_ref[at]
+        return part * jnp.exp2(part[owned : owned + 1] - SUM_HEADROOM)
+
+    outgoing = []
     for q in range(qcount):
         density = []
         for component in range(2):
-            total = parts_ref[q * far * 2 + component].astype(jnp.float32)
+            total = unscaled(q * far * 2 + component)
             for step in range(1, far):
-                total += parts_ref[(q * far + step) * 2 + component].astype(jnp.float32)
-            density.append(total[:, :virtuals])
+                total += unscaled((q * far + step) * 2 + component)
+            density.append(total[:, :virtuals].astype(jnp.bfloat16).astype(jnp.float32))
         real, imag = density
         upper = jnp.concatenate([real, -imag], 1)
         lower = jnp.concatenate([imag, real], 1)
-        rows = jnp.concatenate([upper, lower], 0)
-        high = rows.astype(jnp.bfloat16)
-        low = (rows - high.astype(jnp.float32)).astype(jnp.bfloat16)
-        both = jnp.concatenate([high, low], 0)
-        gamma = jnp.dot(both, factors_ref[q], preferred_element_type=jnp.float32)
-        gamma = gamma[: 2 * SUBLANES] + gamma[2 * SUBLANES :]
+        rows = jnp.concatenate([upper, lower], 0).astype(jnp.bfloat16)
+        gamma = jnp.dot(rows, factors_ref[q], preferred_element_type=jnp.float32)
         for row in range(owned):
-            out_ref[q, row] = jnp.concatenate(
+            held[q, row] = jnp.concatenate(
                 [gamma[row : row + 1], gamma[SUBLANES + row : SUBLANES + row + 1]], 0
             )
+        copy = pltpu.make_async_copy(held.at[q], out_ref.at[q], left.at[q])
+        copy.start()
+        outgoing.append(copy)
+    for copy in outgoing:
+        copy.wait()
 
 
 def factor_product(parts, factors, owned, far):
     qcount, _, columns = factors.shape
+    shape = (qcount, owned, 2, columns)
     return pl.pallas_call(
         lambda *refs: factor_kernel(far, *refs),
-        out_shape=jax.ShapeDtypeStruct((qcount, owned, 2, columns), jnp.float32),
+        out_shape=jax.ShapeDtypeStruct(shape, jnp.float32),
         in_specs=[pl.BlockSpec(memory_space=pltpu.VMEM)] * 2,
-        out_specs=pl.BlockSpec(memory_space=pltpu.VMEM),
+        out_specs=pl.BlockSpec(memory_space=pltpu.HBM),
+        scratch_shapes=[pltpu.VMEM(shape, jnp.float32), pltpu.SemaphoreType.DMA((qcount,))],
         compiler_params=pltpu.CompilerParams(vmem_limit_bytes=24 * 2**20),
         name="factors",
     )(parts, factors)
@@ -243,12 +253,15 @@
     members = [[group * pieces + piece for group in ring for piece in range(pieces)]]
     tiles = partial.reshape(lax.axis_size(near), SUBLANES, LANES).astype(jnp.float16)
     tiles = lax.all_to_all(tiles, near, 0, 0, axis_index_groups=members).astype(jnp.float32)
-    tile = (tiles * jnp.exp2(tiles[:, owned : owned + 1, :] - HEADROOM)).sum(0)
-    tile = tile.astype(jnp.bfloat16)
+    exponents = tiles[:, owned : owned + 1, :]
+    largest = exponents.max(0)
+    tile = (tiles * jnp.exp2(exponents - HEADROOM)).sum(0) * jnp.exp2(SUM_HEADROOM - largest)
+    row = lax.broadcasted_iota(jnp.int32, tile.shape, 0)
+    tile = jnp.where(row < owned, tile, largest).astype(jnp.float16)
     copies = jnp.broadcast_to(tile[None], (lax.axis_size(orb),) + tile.shape)
     half = lax.axis_size(orb) // 4
     order = [[*range(half, 2 * half), *range(half), *range(2 * half, 4 * half)]]
-    parts = lax.all_to_all(copies, orb, 0, 0, axis_index_groups=order)
+    parts = lax.all_to_all(copies, orb, 0, 0, axis_index_groups=order).astype(jnp.float32)
     factors = aux_factor.reshape(qcount, 2 * virtuals, aux_factor.shape[3])
     gamma = factor_product(parts, factors, owned, lax.axis_size("z_hi"))
     return gamma.transpose(0, 2, 1, 3)

time: 70.1 us -> 71.3 us (1.017)
  blocking collectives: 63.4 us -> 51.1 us
  starting transfers between devices: 0 us -> 9.24 us
  waiting for transfers between devices: 0 us -> 3.54 us
  other arithmetic: 0.18 us -> 0.96 us
    all_to_all x2 -> x1, blocking collectives: 31.2 us -> 18.8 us  [local(): lax.all_to_all(copies, orb, 0, 0, axis_index_groups=order)]
    all_to_all x0 -> x1, starting transfers between devices: none -> 9.24 us  [local(): lax.all_to_all(tiles, near, 0, 0, axis_index_groups=members)]
    all_to_all x0 -> x1, waiting for transfers between devices: none -> 3.54 us  [local(): lax.all_to_all(tiles, near, 0, 0, axis_index_groups=members)]
  transfers between devices with their start and end apart: 0 -> 1, of which waited for: 0 -> 1; matrix products, arithmetic and copies ran while one was open for 0% -> 0% of each run, Pallas kernels for 0% -> 0%
where the time goes in v6:
time: 71.3 us; the launch traced here: 70.9 us
  blocking collectives  51.1 us (72%)
  starting transfers between devices  9.24 us (13%)
  Pallas kernels  5.95 us (8%)
  waiting for transfers between devices  3.54 us (5%)
  other arithmetic  0.96 us (1%)
    all_to_all x1, blocking collectives, local(): exchanged = lax.all_to_all(packed, 'kring', 0, 0, axis_index_groups=[ring])  32.3 us
    all_to_all x1, blocking collectives, local(): lax.all_to_all(copies, orb, 0, 0, axis_index_groups=order)  18.8 us
    all_to_all x1, starting transfers between devices, local(): lax.all_to_all(tiles, near, 0, 0, axis_index_groups=members)  9.24 us
    all_to_all x1, waiting for transfers between devices, local(): lax.all_to_all(tiles, near, 0, 0, axis_index_groups=members)  3.54 us
    pallas_call x1, Pallas kernels, pack(): pl.pallas_call(pack_kernel, out_shape=(jax.ShapeDtypeStruct((contracted,...  2.75 us
    pallas_call x1, Pallas kernels, pair_terms(): pl.pallas_call(lambda *refs: pair_kernel(virtuals, ring, *refs), out_shap...  2.13 us
  transfers between devices with their start and end apart: 1, of which 1 were waited for; matrix products, arithmetic and copies ran while one was open for 0% of the time, Pallas kernels for 0%

profile of v6, /device:TPU:1, one launch (start us, length us, event | category | flops | bytes accessed | tf_op | source)
XLA Modules:
  0.0 70.9 jit_solution(4390845975730099863)
XLA Ops:
  0.0 2.8 %pack.1 = (bf16[896,896]{1,0:T(8,128)(2,1)}, s32[32,128]{1,0:T(8,128)}) custom-call(bf16[448,896]{1,0:T(8,128)(2,1)} %bitcast.9, bf16[448,896]{1,0:T(8,128)(2,1)} %bitcast.10, s32[32,32]{1,0:T(8,128)} %table_ref.1), custom_call_target="tpu_custom_call" | custom-call | tf_op jit(solution)/shard_map/pack/pallas_call | solution.py:71
  2.8 0.0 copy-start.1
  2.8 32.3 %all_to_all.15.refs_1_ = bf16[16,56,896]{2,1,0:T(8,128)(2,1)S(1)} all-to-all(bf16[16,56,896]{2,1,0:T(8,128)(2,1)} %bitcast.8), channel_id=1, replica_groups={{416,384,480,448,32,0,96,64,160,128,224,192,288,256,352,320},{417,385,4..., dimensions={0} | all-to-all | bytes 3211264 | tf_op jit(solution)/shard_map/all_to_all | solution.py:248
  35.0 0.0 copy-done.1
  35.0 0.0 copy-start
  35.0 2.1 %pairs.1 = f32[16,32,128]{2,1,0:T(8,128)S(1)} custom-call(s32[32,128]{1,0:T(8,128)S(1)} %copy-done.1, bf16[16,56,896]{2,1,0:T(8,128)(2,1)S(1)} %all_to_all.15.refs_1_), custom_call_target="tpu_custom_call" | custom-call | tf_op jit(solution)/shard_map/pairs/pallas_call | solution.py:171
  37.2 0.7 convert_element_type.19
  37.8 9.2 %all-to-all-start.1 = ((f16[64,8,128]{2,1,0:T(8,128)(2,1)}), f16[64,8,128]{2,1,0:T(8,128)(2,1)S(1)}, u32[]{:S(2)}, u32[]{:S(2)}) async-start(f16[64,8,128]{2,1,0:T(8,128)(2,1)} %bitcast.3), calls=%async_computation.1 | async-start | bytes 262144 | tf_op jit(solution)/shard_map/all_to_all | solution.py:255
  47.1 3.5 %all-to-all-done.1 = f16[64,8,128]{2,1,0:T(8,128)(2,1)S(1)} async-done(((f16[64,8,128]{2,1,0:T(8,128)(2,1)}), f16[64,8,128]{2,1,0:T(8,128)(2,1)S(1)}, u32[]{:S(2)}, u32[]{:S(2)}) %all-to-all-start.1) | async-done | bytes 131104 | tf_op jit(solution)/shard_map/all_to_all | solution.py:255
  50.7 0.1 slice_reduce_fusion
  50.8 0.1 multiply_reduce_fusion
  50.9 0.1 select_convert_fusion
  50.9 18.8 %all_to_all.16 = f16[32,8,128]{2,1,0:T(8,128)(2,1)S(1)} all-to-all(f16[32,8,128]{2,1,0:T(8,128)(2,1)S(1)} %broadcast_in_dim.15), channel_id=1, replica_groups={{8,9,10,11,12,13,14,15,0,1,2,3,4,5,6,7,16,17,18,19,20,21,22,23,24,25,26..., dimensions={0} | all-to-all | bytes 131072 | tf_op jit(solution)/shard_map/all_to_all | solution.py:264
  69.8 0.0 copy-done
  69.8 1.1 %factors.1 = f32[2,7,2,1680]{3,2,1,0:T(2,128)} custom-call(f32[32,8,128]{2,1,0:T(8,128)S(1)} %convert_element_type.23.refs_0_, bf16[2,224,1680]{2,1,0:T(8,128)(2,1)S(1)} %bitcast.7), custom_call_target="tpu_custom_call" | custom-call | tf_op jit(solution)/shard_map/factors/pallas_call | solution.py:224
  (5 shorter events, 0.1 us)
Async XLA Ops:
  2.8 32.3 %copy-start.1 = (s32[32,128]{1,0:T(8,128)S(1)}, s32[32,128]{1,0:T(8,128)}, u32[]{:S(2)}) copy-start(s32[32,128]{1,0:T(8,128)} %get-tuple-element.7.refs_0_) | copy-start | bytes 49156
  35.0 34.8 %copy-start = (bf16[2,2,112,1680]{3,2,1,0:T(8,128)(2,1)S(1)}, bf16[2,2,112,1680]{3,2,1,0:T(8,128)(2,1)}, u32[]{:S(2)}) copy-start(bf16[2,2,112,1680]{3,2,1,0:T(8,128)(2,1)} %param.6) | copy-start | bytes 4515844
  37.8 12.8 %all-to-all-start.1 = ((f16[64,8,128]{2,1,0:T(8,128)(2,1)}), f16[64,8,128]{2,1,0:T(8,128)(2,1)S(1)}, u32[]{:S(2)}, u32[]{:S(2)}) async-start(f16[64,8,128]{2,1,0:T(8,128)(2,1)} %bitcast.3), calls=%async_computation.1 | async-start | bytes 262144 | tf_op jit(solution)/shard_map/all_to_all | solution.py:255

commit v7 on v5

--- a/solution.py
+++ b/solution.py
@@ -26,16 +26,19 @@
     )
 
 
-def pack_kernel(
-    tau_ref, lambda_ref, table_ref, packed_ref, slots_ref, both, turned, table_here, slots_here, arrived, left
-):
-    rows, contracted = tau_ref.shape
-    tiles = contracted // LANES
-    table_copy = pltpu.make_async_copy(table_ref, table_here, arrived.at[2 * tiles])
-    table_copy.start()
+def pack_kernel(first, count, tau_ref, lambda_ref, *refs):
+    if len(refs) == 5:
+        packed_ref, both, turned, arrived, left = refs
+    else:
+        table_ref, packed_ref, slots_ref, both, turned, arrived, left, table_here, slots_here = refs
+    rows = tau_ref.shape[0]
+    outgoing = []
+    if len(refs) > 5:
+        table_copy = pltpu.make_async_copy(table_ref, table_here, arrived.at[2 * count])
+        table_copy.start()
     incoming = []
-    for tile in range(tiles):
-        lanes = pl.ds(tile * LANES, LANES)
+    for tile in range(count):
+        lanes = pl.ds((first + tile) * LANES, LANES)
         for part, source in enumerate((tau_ref, lambda_ref)):
             incoming.append(
                 pltpu.make_async_copy(
@@ -46,12 +49,13 @@
             )
     for copy in incoming:
         copy.start()
-    table_copy.wait()
-    slots_here[...] = partner_slots(table_here[...], slots_here.shape)
-    slots_copy = pltpu.make_async_copy(slots_here, slots_ref, left.at[tiles])
-    slots_copy.start()
-    outgoing = [slots_copy]
-    for tile in range(tiles):
+    if len(refs) > 5:
+        table_copy.wait()
+        slots_here[...] = partner_slots(table_here[...], slots_here.shape)
+        slots_copy = pltpu.make_async_copy(slots_here, slots_ref, left.at[count])
+        slots_copy.start()
+        outgoing.append(slots_copy)
+    for tile in range(count):
         incoming[2 * tile].wait()
         incoming[2 * tile + 1].wait()
         turned[tile] = both[tile].T
@@ -64,33 +68,37 @@
         copy.wait()
 
 
-def pack(tau_rows, lambda_rows, table):
-    rows, contracted = tau_rows.shape
-    tiles = contracted // LANES
+def pack(tau_rows, lambda_rows, first, count, table=None):
+    rows = tau_rows.shape[0]
+    out_shape = [jax.ShapeDtypeStruct((count * LANES, 2 * rows), jnp.bfloat16)]
+    scratch = [
+        pltpu.VMEM((count, 2 * rows, LANES), jnp.bfloat16),
+        pltpu.VMEM((count, LANES, 2 * rows), jnp.bfloat16),
+        pltpu.SemaphoreType.DMA((2 * count + 1,)),
+        pltpu.SemaphoreType.DMA((count + 1,)),
+    ]
+    operands = [tau_rows, lambda_rows]
+    if table is not None:
+        operands.append(table)
+        out_shape.append(jax.ShapeDtypeStruct((table.shape[0], LANES), jnp.int32))
+        scratch.append(pltpu.VMEM(table.shape, jnp.int32))
+        scratch.append(pltpu.VMEM((table.shape[0], LANES), jnp.int32))
+    hbm = pl.BlockSpec(memory_space=pltpu.HBM)
     return pl.pallas_call(
-        pack_kernel,
-        out_shape=(
-            jax.ShapeDtypeStruct((contracted, 2 * rows), jnp.bfloat16),
-            jax.ShapeDtypeStruct((table.shape[0], LANES), jnp.int32),
+        lambda *refs: pack_kernel(first, count, *refs),
+        out_shape=out_shape,
+        in_specs=[hbm] * len(operands),
+        out_specs=[hbm] * len(out_shape),
+        scratch_shapes=scratch,
+        compiler_params=pltpu.CompilerParams(vmem_limit_bytes=56 * 2**20),
+        cost_estimate=pl.CostEstimate(
+            flops=0, bytes_accessed=8 * rows * count * LANES, transcendentals=0
         ),
-        in_specs=[pl.BlockSpec(memory_space=pltpu.HBM)] * 3,
-        out_specs=(pl.BlockSpec(memory_space=pltpu.HBM),) * 2,
-        scratch_shapes=[
-            pltpu.VMEM((tiles, 2 * rows, LANES), jnp.bfloat16),
-            pltpu.VMEM((tiles, LANES, 2 * rows), jnp.bfloat16),
-            pltpu.VMEM(table.shape, jnp.int32),
-            pltpu.VMEM((table.shape[0], LANES), jnp.int32),
-            pltpu.SemaphoreType.DMA((2 * tiles + 1,)),
-            pltpu.SemaphoreType.DMA((tiles + 1,)),
-        ],
-        compiler_params=pltpu.CompilerParams(vmem_limit_bytes=56 * 2**20),
         name="pack",
-    )(tau_rows, lambda_rows, table)
-
-
-def pair_kernel(
-    virtuals, ring, slots_ref, packed_ref, out_ref, tau_part, lambda_part, chosen, slots, arrived
-):
+    )(*operands)
+
+
+def pair_pieces(virtuals, ring, slots_ref, packed_ref, tau_part, lambda_part, chosen, slots, arrived):
     slots_copy = pltpu.make_async_copy(slots_ref, slots, arrived)
     slots_copy.start()
     groups, depth, width = packed_ref.shape
@@ -98,49 +106,43 @@
     slot_rows = tau_part.shape[1]
     qcount = 2
     half = width // 2
-    fill = jnp.zeros((slot_rows - depth, half), jnp.float32)
     lane_fill = jnp.zeros((slot_rows, LANES - virtuals), jnp.bfloat16)
     for place, group in enumerate(ring):
-        block = packed_ref[place].astype(jnp.float32)
-        tau_block = jnp.concatenate([block[:, :half], fill], 0).astype(jnp.bfloat16)
-        lambda_block = jnp.concatenate([block[:, half:], fill], 0).astype(jnp.bfloat16)
+        block = packed_ref[place]
+        if slot_rows > depth:
+            fill = jnp.zeros((slot_rows - depth, width), jnp.float32)
+            block = jnp.concatenate([block.astype(jnp.float32), fill], 0).astype(jnp.bfloat16)
         for local_triple in range(2):
             start = local_triple * 2 * virtuals
-            tau_part[2 * group + local_triple] = tau_block[:, start : start + 2 * virtuals]
+            tau_part[2 * group + local_triple] = block[:, start : start + 2 * virtuals]
+            start += half
             lambda_part[2 * group + local_triple] = jnp.concatenate(
                 [
-                    lambda_block[:, start : start + virtuals],
+                    block[:, start : start + virtuals],
                     lane_fill,
-                    lambda_block[:, start + virtuals : start + 2 * virtuals],
+                    block[:, start + virtuals : start + 2 * virtuals],
                     lane_fill,
                 ],
                 1,
             )
-
     slots_copy.wait()
-
-    def choose(slot, triple):
-        value = lambda_part[slots[triple, slot]]
-        transfer = slots[triple, 2 + slot]
-        for q in range(qcount):
-            lane = (slot * qcount + q) * 2 * LANES
-            chosen[triple, :, lane : lane + 2 * LANES] = jnp.where(
-                transfer == q, value, jnp.zeros_like(value)
-            )
-
     for triple in range(triples):
-        choose(0, triple)
-        choose(1, triple)
-    tau_all = tau_part[...].reshape(triples * slot_rows, 2 * virtuals)
+        for slot in range(2):
+            value = lambda_part[slots[triple, slot]]
+            transfer = slots[triple, 2 + slot]
+            for q in range(qcount):
+                lane = (slot * qcount + q) * 2 * LANES
+                chosen[triple, :, lane : lane + 2 * LANES] = jnp.where(
+                    transfer == q, value, jnp.zeros_like(value)
+                )
     wide = qcount * 2 * LANES
     products = lax.dot_general(
-        tau_all,
+        tau_part[...].reshape(triples * slot_rows, 2 * virtuals),
         chosen[...].reshape(triples * slot_rows, 2 * wide),
         (((0,), (0,)), ((), ())),
         preferred_element_type=jnp.float32,
     )
     total = products[:, :wide] + products[:, wide:]
-    owned = virtuals // groups
     pieces = []
     for q in range(qcount):
         lane = q * 2 * LANES
@@ -148,6 +150,20 @@
         imag_lambda = total[:, lane + LANES : lane + 2 * LANES]
         pieces.append(real_lambda[:virtuals] + imag_lambda[virtuals:])
         pieces.append(real_lambda[virtuals:] - imag_lambda[:virtuals])
+    return pieces
+
+
+def early_kernel(virtuals, ring, slots_ref, packed_ref, out_ref, *scratch):
+    pieces = pair_pieces(virtuals, ring, slots_ref, packed_ref, *scratch)
+    for number, piece in enumerate(pieces):
+        out_ref[number] = piece
+
+
+def late_kernel(virtuals, ring, slots_ref, packed_ref, early_ref, out_ref, *scratch):
+    groups = packed_ref.shape[0]
+    pieces = pair_pieces(virtuals, ring, slots_ref, packed_ref, *scratch)
+    pieces = [piece + early_ref[number] for number, piece in enumerate(pieces)]
+    owned = virtuals // groups
     largest = jnp.abs(pieces[0])
     for piece in pieces[1:]:
         largest = jnp.maximum(largest, jnp.abs(piece))
@@ -163,15 +179,24 @@
             ).astype(out_ref.dtype)
 
 
-def pair_terms(slots, packed, virtuals, ring):
+def pair_terms(slots, packed, virtuals, ring, early=None):
     groups, depth, width = packed.shape
     slot_rows = -(-depth // 16) * 16
     triples = 2 * groups
+    vmem = pl.BlockSpec(memory_space=pltpu.VMEM)
+    operands = [slots, packed]
+    if early is None:
+        kernel = early_kernel
+        shape = (4, virtuals, LANES)
+    else:
+        operands.append(early)
+        kernel = late_kernel
+        shape = (groups, 4 * SUBLANES, LANES)
     return pl.pallas_call(
-        lambda *refs: pair_kernel(virtuals, ring, *refs),
-        out_shape=jax.ShapeDtypeStruct((groups, 4 * SUBLANES, LANES), jnp.float32),
-        in_specs=[pl.BlockSpec(memory_space=pl.ANY), pl.BlockSpec(memory_space=pltpu.VMEM)],
-        out_specs=pl.BlockSpec(memory_space=pltpu.VMEM),
+        lambda *refs: kernel(virtuals, ring, *refs),
+        out_shape=jax.ShapeDtypeStruct(shape, jnp.float32),
+        in_specs=[pl.BlockSpec(memory_space=pl.ANY)] + [vmem] * (len(operands) - 1),
+        out_specs=vmem,
         scratch_shapes=[
             pltpu.VMEM((triples, slot_rows, 2 * virtuals), jnp.bfloat16),
             pltpu.VMEM((triples, slot_rows, 2 * LANES), jnp.bfloat16),
@@ -180,8 +205,13 @@
             pltpu.SemaphoreType.DMA,
         ],
         compiler_params=pltpu.CompilerParams(vmem_limit_bytes=40 * 2**20),
+        cost_estimate=pl.CostEstimate(
+            flops=32 * triples * slot_rows * virtuals * LANES,
+            bytes_accessed=2 * groups * depth * width,
+            transcendentals=0,
+        ),
         name="pairs",
-    )(slots, packed)
+    )(*operands)
 
 
 def factor_kernel(far, parts_ref, factors_ref, out_ref):
@@ -229,14 +259,23 @@
     qcount = aux_factor.shape[0]
     rows = tau_slabs.shape[0] * 2 * virtuals
     owned = virtuals // groups
-    packed, slots = pack(
-        tau_slabs.reshape(rows, contracted), lambda_slabs.reshape(rows, contracted), transfer_table
-    )
-    packed = packed.reshape(groups, contracted // groups, 2 * rows)
+    tau_rows = tau_slabs.reshape(rows, contracted)
+    lambda_rows = lambda_slabs.reshape(rows, contracted)
+    tiles = contracted // LANES
+    split = -(-tiles // 2)
     start = groups - groups // 4
     ring = [group ^ 1 for group in [*range(start, groups), *range(start)]]
-    exchanged = lax.all_to_all(packed, "kring", 0, 0, axis_index_groups=[ring])
-    partial = pair_terms(slots, exchanged, virtuals, ring)
+
+    def exchanged(packed):
+        packed = packed.reshape(groups, packed.shape[0] // groups, 2 * rows)
+        return lax.all_to_all(packed, "kring", 0, 0, axis_index_groups=[ring])
+
+    packed, slots = pack(tau_rows, lambda_rows, 0, split, transfer_table)
+    first = exchanged(packed)
+    (packed,) = pack(tau_rows, lambda_rows, split, tiles - split)
+    second = exchanged(packed)
+    early = pair_terms(slots, first, virtuals, ring)
+    partial = pair_terms(slots, second, virtuals, ring, early)
     near = ("kring", "y_lo", "z_lo")
     orb = ("y_lo", "z_hi", "z_lo")
     pieces = lax.axis_size(near) // groups

time: 70.1 us -> 78.6 us (1.12)
  blocking collectives: 63.4 us -> 31.2 us
  starting transfers between devices: 0 us -> 21.4 us
  waiting for transfers between devices: 0 us -> 16.2 us
  Pallas kernels: 6.01 us -> 9.03 us
    all_to_all x1 -> x0, blocking collectives: 32.3 us -> none  [local(): exchanged = lax.all_to_all(packed, 'kring', 0, 0, axis_index_groups=[ring])]
    all_to_all x0 -> x2, starting transfers between devices: none -> 21.4 us  [exchanged(): return lax.all_to_all(packed, 'kring', 0, 0, axis_index_groups=[ring])]
    all_to_all x0 -> x2, waiting for transfers between devices: none -> 16.2 us  [exchanged(): return lax.all_to_all(packed, 'kring', 0, 0, axis_index_groups=[ring])]
    pallas_call x2 -> x4, Pallas kernels: 4.88 us -> 7.9 us  [the longest x2 4.39 us: pack(): pl.pallas_call(lambda *refs: pack_kernel(first, count, *refs), out_shape=...]
  transfers between devices with their start and end apart: 0 -> 2, of which waited for: 0 -> 2; matrix products, arithmetic and copies ran while one was open for 0% -> 0% of each run, Pallas kernels for 0% -> 5%
where the time goes in v7:
time: 78.6 us; the launch traced here: 78.1 us
  blocking collectives  31.2 us (40%)
  starting transfers between devices  21.4 us (27%)
  waiting for transfers between devices  16.2 us (21%)
  Pallas kernels  9.03 us (11%)
    all_to_all x2, starting transfers between devices, exchanged(): return lax.all_to_all(packed, 'kring', 0, 0, axis_index_groups=[ring])  21.4 us
    all_to_all x1, blocking collectives, local(): parts = lax.all_to_all(copies, orb, 0, 0, axis_index_groups=order)  19.6 us
    all_to_all x2, waiting for transfers between devices, exchanged(): return lax.all_to_all(packed, 'kring', 0, 0, axis_index_groups=[ring])  16.2 us
    all_to_all x1, blocking collectives, local(): lax.all_to_all(tiles, near, 0, 0, axis_index_groups=members)  11.6 us
    pallas_call x2, Pallas kernels, pack(): pl.pallas_call(lambda *refs: pack_kernel(first, count, *refs), out_shape=...  4.39 us
    pallas_call x2, Pallas kernels, pair_terms(): pl.pallas_call(lambda *refs: kernel(virtuals, ring, *refs), out_shape=jax...  3.5 us
  transfers between devices with their start and end apart: 2, of which 2 were waited for; matrix products, arithmetic and copies ran while one was open for 0% of the time, Pallas kernels for 5%

profile of v7, /device:TPU:1, one launch (start us, length us, event | category | flops | bytes accessed | tf_op | source)
XLA Modules:
  0.0 78.1 jit_solution(8173370675834489721)
XLA Ops:
  0.0 2.3 %pack.2 = (bf16[512,896]{1,0:T(8,128)(2,1)}, s32[32,128]{1,0:T(8,128)}) custom-call(bf16[448,896]{1,0:T(8,128)(2,1)} %bitcast.9, bf16[448,896]{1,0:T(8,128)(2,1)} %bitcast.11, s32[32,32]{1,0:T(8,128)} %refs_2_.1), custom_call_target="tpu_custom_call" | custom-call | bytes 1835008 | tf_op jit(solution)/shard_map/pack/pallas_call | solution.py:87
  2.3 13.4 %all-to-all-start.1 = ((bf16[16,32,896]{2,1,0:T(8,128)(2,1)}), bf16[16,32,896]{2,1,0:T(8,128)(2,1)S(1)}, u32[]{:S(2)}, u32[]{:S(2)}) async-start(bf16[16,32,896]{2,1,0:T(8,128)(2,1)} %bitcast.14), calls=%async_computation.1 | async-start | bytes 1835008 | tf_op jit(solution)/shard_map/all_to_all | solution.py:271
  15.7 0.0 copy-start.1
  15.7 2.1 %pack.3 = bf16[384,896]{1,0:T(8,128)(2,1)} custom-call(bf16[448,896]{1,0:T(8,128)(2,1)} %bitcast.10, bf16[448,896]{1,0:T(8,128)(2,1)} %bitcast.12), custom_call_target="tpu_custom_call" | custom-call | bytes 1376256 | tf_op jit(solution)/shard_map/pack/pallas_call | solution.py:87
  17.9 9.0 %all-to-all-done.1.refs_1_ = bf16[16,32,896]{2,1,0:T(8,128)(2,1)S(1)} async-done(((bf16[16,32,896]{2,1,0:T(8,128)(2,1)}), bf16[16,32,896]{2,1,0:T(8,128)(2,1)S(1)}, u32[]{:S(2)}, u32[]{:S(2)}) %all-to-all-start.1) | async-done | bytes 917536 | tf_op jit(solution)/shard_map/all_to_all | solution.py:271
  26.9 7.9 %all-to-all-start = ((bf16[16,24,896]{2,1,0:T(8,128)(2,1)}), bf16[16,24,896]{2,1,0:T(8,128)(2,1)S(1)}, u32[]{:S(2)}, u32[]{:S(2)}) async-start(bf16[16,24,896]{2,1,0:T(8,128)(2,1)} %bitcast.13), calls=%async_computation | async-start | bytes 1376256 | tf_op jit(solution)/shard_map/all_to_all | solution.py:271
  34.8 0.0 copy-done.1
  34.8 1.5 %pairs.2.refs_2_ = f32[4,112,128]{2,1,0:T(8,128)S(1)} custom-call(s32[32,128]{1,0:T(8,128)S(1)} %copy-done.1, bf16[16,32,896]{2,1,0:T(8,128)(2,1)S(1)} %all-to-all-done.1.refs_1_), custom_call_target="tpu_custom_call" | custom-call | flops 469762048 | bytes 917504 | tf_op jit(solution)/shard_map/pairs/pallas_call | solution.py:195
  36.3 0.0 copy-start
  36.3 7.2 %all-to-all-done.refs_1_ = bf16[16,24,896]{2,1,0:T(8,128)(2,1)S(1)} async-done(((bf16[16,24,896]{2,1,0:T(8,128)(2,1)}), bf16[16,24,896]{2,1,0:T(8,128)(2,1)S(1)}, u32[]{:S(2)}, u32[]{:S(2)}) %all-to-all-start) | async-done | bytes 688160 | tf_op jit(solution)/shard_map/all_to_all | solution.py:271
  43.5 2.0 %pairs.3 = f32[16,32,128]{2,1,0:T(8,128)S(1)} custom-call(s32[32,128]{1,0:T(8,128)S(1)} %copy-done.1, bf16[16,24,896]{2,1,0:T(8,128)(2,1)S(1)} %all-to-all-done.refs_1_, f32[4,112,128]{2,1,0:T(8,128)S(1)} %pairs.2.refs_2_), custom_call_target="tpu_custom_call" | custom-call | flops 469762048 | bytes 688128 | tf_op jit(solution)/shard_map/pairs/pallas_call | solution.py:195
  45.6 11.6 %all_to_all.20 = f16[64,8,128]{2,1,0:T(8,128)(2,1)S(1)} all-to-all(f16[64,8,128]{2,1,0:T(8,128)(2,1)S(1)} %bitcast.15), channel_id=1, replica_groups={{416,417,432,433,384,385,400,401,480,481,496,497,448,449,464,465,32,33,..., dimensions={0} | all-to-all | bytes 262144 | tf_op jit(solution)/shard_map/all_to_all | solution.py:284
  57.2 0.1 fusion.1
  57.3 0.1 multiply_reduce_fusion
  57.4 19.6 %all_to_all.21.refs_0_ = bf16[32,8,128]{2,1,0:T(8,128)(2,1)S(1)} all-to-all(bf16[32,8,128]{2,1,0:T(8,128)(2,1)S(1)} %broadcast_in_dim.2), channel_id=1, replica_groups={{8,9,10,11,12,13,14,15,0,1,2,3,4,5,6,7,16,17,18,19,20,21,22,23,24,25,26..., dimensions={0} | all-to-all | bytes 131072 | tf_op jit(solution)/shard_map/all_to_all | solution.py:290
  76.9 0.0 copy-done
  76.9 1.1 %factors.1 = f32[2,7,2,1680]{3,2,1,0:T(2,128)} custom-call(bf16[32,8,128]{2,1,0:T(8,128)(2,1)S(1)} %all_to_all.21.refs_0_, bf16[2,224,1680]{2,1,0:T(8,128)(2,1)S(1)} %bitcast.8), custom_call_target="tpu_custom_call" | custom-call | tf_op jit(solution)/shard_map/factors/pallas_call | solution.py:245
  (3 shorter events, 0.1 us)
Async XLA Ops:
  2.3 24.6 %all-to-all-start.1 = ((bf16[16,32,896]{2,1,0:T(8,128)(2,1)}), bf16[16,32,896]{2,1,0:T(8,128)(2,1)S(1)}, u32[]{:S(2)}, u32[]{:S(2)}) async-start(bf16[16,32,896]{2,1,0:T(8,128)(2,1)} %bitcast.14), calls=%async_computation.1 | async-start | bytes 1835008 | tf_op jit(solution)/shard_map/all_to_all | solution.py:271
  15.7 19.1 %copy-start.1 = (s32[32,128]{1,0:T(8,128)S(1)}, s32[32,128]{1,0:T(8,128)}, u32[]{:S(2)}) copy-start(s32[32,128]{1,0:T(8,128)} %get-tuple-element.7.refs_0_) | copy-start | bytes 49156
  26.9 16.7 %all-to-all-start = ((bf16[16,24,896]{2,1,0:T(8,128)(2,1)}), bf16[16,24,896]{2,1,0:T(8,128)(2,1)S(1)}, u32[]{:S(2)}, u32[]{:S(2)}) async-start(bf16[16,24,896]{2,1,0:T(8,128)(2,1)} %bitcast.13), calls=%async_computation | async-start | bytes 1376256 | tf_op jit(solution)/shard_map/all_to_all | solution.py:271
  36.3 40.6 %copy-start = (bf16[2,2,112,1680]{3,2,1,0:T(8,128)(2,1)S(1)}, bf16[2,2,112,1680]{3,2,1,0:T(8,128)(2,1)}, u32[]{:S(2)}) copy-start(bf16[2,2,112,1680]{3,2,1,0:T(8,128)(2,1)} %param.6) | copy-start | bytes 4515844

commit v8 on v6

--- a/solution.py
+++ b/solution.py
@@ -256,8 +256,7 @@
     exponents = tiles[:, owned : owned + 1, :]
     largest = exponents.max(0)
     tile = (tiles * jnp.exp2(exponents - HEADROOM)).sum(0) * jnp.exp2(SUM_HEADROOM - largest)
-    row = lax.broadcasted_iota(jnp.int32, tile.shape, 0)
-    tile = jnp.where(row < owned, tile, largest).astype(jnp.float16)
+    tile = jnp.concatenate([tile[:owned], largest], 0).astype(jnp.float16)
     copies = jnp.broadcast_to(tile[None], (lax.axis_size(orb),) + tile.shape)
     half = lax.axis_size(orb) // 4
     order = [[*range(half, 2 * half), *range(half), *range(2 * half, 4 * half)]]

time: 71.3 us -> 70.1 us (0.983)
  blocking collectives: 51.1 us -> 63.4 us
  starting transfers between devices: 9.24 us -> 0 us
  waiting for transfers between devices: 3.54 us -> 0 us
  other arithmetic: 0.96 us -> 0.24 us
    all_to_all x0 -> x1, blocking collectives: none -> 12 us  [local(): lax.all_to_all(tiles, near, 0, 0, axis_index_groups=members)]
    all_to_all x1 -> x0, starting transfers between devices: 9.24 us -> none  [local(): lax.all_to_all(tiles, near, 0, 0, axis_index_groups=members)]
    all_to_all x1 -> x0, waiting for transfers between devices: 3.54 us -> none  [local(): lax.all_to_all(tiles, near, 0, 0, axis_index_groups=members)]
  transfers between devices with their start and end apart: 1 -> 0, of which waited for: 1 -> 0; matrix products, arithmetic and copies ran while one was open for 0% -> 0% of each run, Pallas kernels for 0% -> 0%
where the time goes in v8:
time: 70.1 us; the launch traced here: 69.7 us
  blocking collectives  63.4 us (90%)
  Pallas kernels  5.95 us (8%)
    all_to_all x1, blocking collectives, local(): exchanged = lax.all_to_all(packed, 'kring', 0, 0, axis_index_groups=[ring])  32.3 us
    all_to_all x1, blocking collectives, local(): lax.all_to_all(copies, orb, 0, 0, axis_index_groups=order)  19.2 us
    all_to_all x1, blocking collectives, local(): lax.all_to_all(tiles, near, 0, 0, axis_index_groups=members)  12 us
    pallas_call x1, Pallas kernels, pack(): pl.pallas_call(pack_kernel, out_shape=(jax.ShapeDtypeStruct((contracted,...  2.76 us
    pallas_call x1, Pallas kernels, pair_terms(): pl.pallas_call(lambda *refs: pair_kernel(virtuals, ring, *refs), out_shap...  2.13 us

profile of v8, /device:TPU:1, one launch (start us, length us, event | category | flops | bytes accessed | tf_op | source)
XLA Modules:
  0.0 69.7 jit_solution(15204359199005610356)
XLA Ops:
  0.0 2.8 %pack.1 = (bf16[896,896]{1,0:T(8,128)(2,1)}, s32[32,128]{1,0:T(8,128)}) custom-call(bf16[448,896]{1,0:T(8,128)(2,1)} %bitcast.12, bf16[448,896]{1,0:T(8,128)(2,1)} %bitcast.13, s32[32,32]{1,0:T(8,128)} %table_ref.1), custom_call_target="tpu_custom_call" | custom-call | tf_op jit(solution)/shard_map/pack/pallas_call | solution.py:71
  2.8 0.0 copy-start.1
  2.8 32.3 %all_to_all.15.refs_1_ = bf16[16,56,896]{2,1,0:T(8,128)(2,1)S(1)} all-to-all(bf16[16,56,896]{2,1,0:T(8,128)(2,1)} %bitcast.11), channel_id=1, replica_groups={{416,384,480,448,32,0,96,64,160,128,224,192,288,256,352,320},{417,385,4..., dimensions={0} | all-to-all | bytes 3211264 | tf_op jit(solution)/shard_map/all_to_all | solution.py:248
  35.0 0.0 copy-done.1
  35.0 0.0 copy-start
  35.0 2.1 %pairs.1 = f32[16,32,128]{2,1,0:T(8,128)S(1)} custom-call(s32[32,128]{1,0:T(8,128)S(1)} %copy-done.1, bf16[16,56,896]{2,1,0:T(8,128)(2,1)S(1)} %all_to_all.15.refs_1_), custom_call_target="tpu_custom_call" | custom-call | tf_op jit(solution)/shard_map/pairs/pallas_call | solution.py:171
  37.2 12.0 %all_to_all.16 = f16[64,8,128]{2,1,0:T(8,128)(2,1)S(1)} all-to-all(f16[64,8,128]{2,1,0:T(8,128)(2,1)S(1)} %bitcast.14), channel_id=1, replica_groups={{416,417,432,433,384,385,400,401,480,481,496,497,448,449,464,465,32,33,..., dimensions={0} | all-to-all | bytes 262144 | tf_op jit(solution)/shard_map/all_to_all | solution.py:255
  49.2 0.1 multiply_exponential_fusion
  49.3 0.1 multiply_reduce_fusion
  49.4 19.2 %all_to_all.17 = f16[32,8,128]{2,1,0:T(8,128)(2,1)S(1)} all-to-all(f16[32,8,128]{2,1,0:T(8,128)(2,1)S(1)} %broadcast_in_dim.2), channel_id=1, replica_groups={{8,9,10,11,12,13,14,15,0,1,2,3,4,5,6,7,16,17,18,19,20,21,22,23,24,25,26..., dimensions={0} | all-to-all | bytes 131072 | tf_op jit(solution)/shard_map/all_to_all | solution.py:263
  68.6 0.0 copy-done
  68.6 1.1 %factors.1 = f32[2,7,2,1680]{3,2,1,0:T(2,128)} custom-call(f32[32,8,128]{2,1,0:T(8,128)S(1)} %convert_element_type.20.refs_0_, bf16[2,224,1680]{2,1,0:T(8,128)(2,1)S(1)} %bitcast.10), custom_call_target="tpu_custom_call" | custom-call | tf_op jit(solution)/shard_map/factors/pallas_call | solution.py:224
  (7 shorter events, 0.1 us)
Async XLA Ops:
  2.8 32.3 %copy-start.1 = (s32[32,128]{1,0:T(8,128)S(1)}, s32[32,128]{1,0:T(8,128)}, u32[]{:S(2)}) copy-start(s32[32,128]{1,0:T(8,128)} %get-tuple-element.7.refs_0_) | copy-start | bytes 49156
  35.0 33.6 %copy-start = (bf16[2,2,112,1680]{3,2,1,0:T(8,128)(2,1)S(1)}, bf16[2,2,112,1680]{3,2,1,0:T(8,128)(2,1)}, u32[]{:S(2)}) copy-start(bf16[2,2,112,1680]{3,2,1,0:T(8,128)(2,1)} %param.6) | copy-start | bytes 4515844

commit v9 on v8

--- a/solution.py
+++ b/solution.py
@@ -28,7 +28,7 @@
 
 
 def pack_kernel(
-    tau_ref, lambda_ref, table_ref, packed_ref, slots_ref, both, turned, table_here, slots_here, arrived, left
+    tau_ref, lambda_ref, table_ref, packed_ref, slots_ref, both, table_here, slots_here, arrived, left
 ):
     rows, contracted = tau_ref.shape
     tiles = contracted // LANES
@@ -49,18 +49,13 @@
         copy.start()
     table_copy.wait()
     slots_here[...] = partner_slots(table_here[...], slots_here.shape)
-    slots_copy = pltpu.make_async_copy(slots_here, slots_ref, left.at[tiles])
+    slots_copy = pltpu.make_async_copy(slots_here, slots_ref, left)
     slots_copy.start()
     outgoing = [slots_copy]
     for tile in range(tiles):
         incoming[2 * tile].wait()
         incoming[2 * tile + 1].wait()
-        turned[tile] = both[tile].T
-        copy = pltpu.make_async_copy(
-            turned.at[tile], packed_ref.at[pl.ds(tile * LANES, LANES)], left.at[tile]
-        )
-        copy.start()
-        outgoing.append(copy)
+        packed_ref[tile * LANES : (tile + 1) * LANES] = both[tile].T
     for copy in outgoing:
         copy.wait()
 
@@ -75,18 +70,17 @@
             jax.ShapeDtypeStruct((table.shape[0], LANES), jnp.int32),
         ),
         in_specs=[pl.BlockSpec(memory_space=pltpu.HBM)] * 3,
-        out_specs=(pl.BlockSpec(memory_space=pltpu.HBM),) * 2,
+        out_specs=(pl.BlockSpec(memory_space=pltpu.VMEM), pl.BlockSpec(memory_space=pltpu.HBM)),
         scratch_shapes=[
             pltpu.VMEM((tiles, 2 * rows, LANES), jnp.bfloat16),
-            pltpu.VMEM((tiles, LANES, 2 * rows), jnp.bfloat16),
             pltpu.VMEM(table.shape, jnp.int32),
             pltpu.VMEM((table.shape[0], LANES), jnp.int32),
             pltpu.SemaphoreType.DMA((2 * tiles + 1,)),
-            pltpu.SemaphoreType.DMA((tiles + 1,)),
+            pltpu.SemaphoreType.DMA,
         ],
-        compiler_params=pltpu.CompilerParams(vmem_limit_bytes=56 * 2**20),
+        compiler_params=pltpu.CompilerParams(vmem_limit_bytes=16 * 2**20),
         name="pack",
-    )(tau_rows, lambda_rows, table)
+    )(*(pltpu.with_memory_space_constraint(x, pltpu.HBM) for x in (tau_rows, lambda_rows, table)))
 
 
 def pair_kernel(

time: 70.1 us -> 69 us (0.984)
  Pallas kernels: 5.95 us -> 5.2 us
    pallas_call x1, Pallas kernels: 2.76 us -> 2.01 us  [pack(): pl.pallas_call(pack_kernel, out_shape=(jax.ShapeDtypeStruct((contracted,...]
where the time goes in v9:
time: 69 us; the launch traced here: 68.7 us
  blocking collectives  63.1 us (91%)
  Pallas kernels  5.2 us (8%)
    all_to_all x1, blocking collectives, local(): exchanged = lax.all_to_all(packed, 'kring', 0, 0, axis_index_groups=[ring])  32 us
    all_to_all x1, blocking collectives, local(): lax.all_to_all(copies, orb, 0, 0, axis_index_groups=order)  19.1 us
    all_to_all x1, blocking collectives, local(): lax.all_to_all(tiles, near, 0, 0, axis_index_groups=members)  12 us
    pallas_call x1, Pallas kernels, pair_terms(): pl.pallas_call(lambda *refs: pair_kernel(virtuals, ring, *refs), out_shap...  2.13 us
    pallas_call x1, Pallas kernels, pack(): pl.pallas_call(pack_kernel, out_shape=(jax.ShapeDtypeStruct((contracted,...  2.01 us

profile of v9, /device:TPU:1, one launch (start us, length us, event | category | flops | bytes accessed | tf_op | source)
XLA Modules:
  0.0 68.7 jit_solution(15638151320888350017)
XLA Ops:
  0.0 2.0 %pack.1 = (bf16[896,896]{1,0:T(8,128)(2,1)S(1)}, s32[32,128]{1,0:T(8,128)S(1)}) custom-call(bf16[448,896]{1,0:T(8,128)(2,1)} %bitcast.12, bf16[448,896]{1,0:T(8,128)(2,1)} %bitcast.13, s32[32,32]{1,0:T(8,128)} %table_ref.1), custom_call_target="tpu_custom_call" | custom-call | tf_op jit(solution)/shard_map/pack/pallas_call | solution.py:66
  2.0 32.0 %all_to_all.15.refs_1_ = bf16[16,56,896]{2,1,0:T(8,128)(2,1)S(1)} all-to-all(bf16[16,56,896]{2,1,0:T(8,128)(2,1)S(1)} %bitcast.11), channel_id=1, replica_groups={{416,384,480,448,32,0,96,64,160,128,224,192,288,256,352,320},{417,385,4..., dimensions={0} | all-to-all | bytes 3211264 | tf_op jit(solution)/shard_map/all_to_all | solution.py:242
  34.1 0.0 copy-start
  34.1 2.1 %pairs.1 = f32[16,32,128]{2,1,0:T(8,128)S(1)} custom-call(s32[32,128]{1,0:T(8,128)S(1)} %get-tuple-element.7.refs_0_, bf16[16,56,896]{2,1,0:T(8,128)(2,1)S(1)} %all_to_all.15.refs_1_), custom_call_target="tpu_custom_call" | custom-call | tf_op jit(solution)/shard_map/pairs/pallas_call | solution.py:165
  36.2 12.0 %all_to_all.16 = f16[64,8,128]{2,1,0:T(8,128)(2,1)S(1)} all-to-all(f16[64,8,128]{2,1,0:T(8,128)(2,1)S(1)} %bitcast.14), channel_id=1, replica_groups={{416,417,432,433,384,385,400,401,480,481,496,497,448,449,464,465,32,33,..., dimensions={0} | all-to-all | bytes 262144 | tf_op jit(solution)/shard_map/all_to_all | solution.py:249
  48.2 0.1 multiply_exponential_fusion
  48.3 0.1 multiply_reduce_fusion
  48.4 19.1 %all_to_all.17 = f16[32,8,128]{2,1,0:T(8,128)(2,1)S(1)} all-to-all(f16[32,8,128]{2,1,0:T(8,128)(2,1)S(1)} %broadcast_in_dim.2), channel_id=1, replica_groups={{8,9,10,11,12,13,14,15,0,1,2,3,4,5,6,7,16,17,18,19,20,21,22,23,24,25,26..., dimensions={0} | all-to-all | bytes 131072 | tf_op jit(solution)/shard_map/all_to_all | solution.py:257
  67.6 0.0 copy-done
  67.6 1.1 %factors.1 = f32[2,7,2,1680]{3,2,1,0:T(2,128)} custom-call(f32[32,8,128]{2,1,0:T(8,128)S(1)} %convert_element_type.20.refs_0_, bf16[2,224,1680]{2,1,0:T(8,128)(2,1)S(1)} %bitcast.10), custom_call_target="tpu_custom_call" | custom-call | tf_op jit(solution)/shard_map/factors/pallas_call | solution.py:218
  (7 shorter events, 0.1 us)
Async XLA Ops:
  34.1 33.5 %copy-start = (bf16[2,2,112,1680]{3,2,1,0:T(8,128)(2,1)S(1)}, bf16[2,2,112,1680]{3,2,1,0:T(8,128)(2,1)}, u32[]{:S(2)}) copy-start(bf16[2,2,112,1680]{3,2,1,0:T(8,128)(2,1)} %param.6) | copy-start | bytes 4515844

commit v10 on v9

--- a/solution.py
+++ b/solution.py
@@ -28,7 +28,7 @@
 
 
 def pack_kernel(
-    tau_ref, lambda_ref, table_ref, packed_ref, slots_ref, both, table_here, slots_here, arrived, left
+    tau_ref, lambda_ref, table_ref, packed_ref, slots_ref, both, table_here, arrived
 ):
     rows, contracted = tau_ref.shape
     tiles = contracted // LANES
@@ -48,16 +48,11 @@
     for copy in incoming:
         copy.start()
     table_copy.wait()
-    slots_here[...] = partner_slots(table_here[...], slots_here.shape)
-    slots_copy = pltpu.make_async_copy(slots_here, slots_ref, left)
-    slots_copy.start()
-    outgoing = [slots_copy]
+    slots_ref[...] = partner_slots(table_here[...], slots_ref.shape)
     for tile in range(tiles):
         incoming[2 * tile].wait()
         incoming[2 * tile + 1].wait()
         packed_ref[tile * LANES : (tile + 1) * LANES] = both[tile].T
-    for copy in outgoing:
-        copy.wait()
 
 
 def pack(tau_rows, lambda_rows, table):
@@ -70,13 +65,11 @@
             jax.ShapeDtypeStruct((table.shape[0], LANES), jnp.int32),
         ),
         in_specs=[pl.BlockSpec(memory_space=pltpu.HBM)] * 3,
-        out_specs=(pl.BlockSpec(memory_space=pltpu.VMEM), pl.BlockSpec(memory_space=pltpu.HBM)),
+        out_specs=(pl.BlockSpec(memory_space=pltpu.VMEM),) * 2,
         scratch_shapes=[
             pltpu.VMEM((tiles, 2 * rows, LANES), jnp.bfloat16),
             pltpu.VMEM(table.shape, jnp.int32),
-            pltpu.VMEM((table.shape[0], LANES), jnp.int32),
             pltpu.SemaphoreType.DMA((2 * tiles + 1,)),
-            pltpu.SemaphoreType.DMA,
         ],
         compiler_params=pltpu.CompilerParams(vmem_limit_bytes=16 * 2**20),
         name="pack",
@@ -252,8 +245,9 @@
     tile = (tiles * jnp.exp2(exponents - HEADROOM)).sum(0) * jnp.exp2(SUM_HEADROOM - largest)
     tile = jnp.concatenate([tile[:owned], largest], 0).astype(jnp.float16)
     copies = jnp.broadcast_to(tile[None], (lax.axis_size(orb),) + tile.shape)
-    half = lax.axis_size(orb) // 4
-    order = [[*range(half, 2 * half), *range(half), *range(2 * half, 4 * half)]]
+    depth = lax.axis_size(orb) // 2
+    late = depth * 5 // 8
+    order = [[*range(late, depth), *range(late), *range(depth, 2 * depth)]]
     parts = lax.all_to_all(copies, orb, 0, 0, axis_index_groups=order).astype(jnp.float32)
     factors = aux_factor.reshape(qcount, 2 * virtuals, aux_factor.shape[3])
     gamma = factor_product(parts, factors, owned, lax.axis_size("z_hi"))

time: 69 us -> 69 us (level)
  no operation moved by 1% of the time
where the time goes in v10:
time: 69 us; the launch traced here: 68.6 us
  blocking collectives  63.1 us (91%)
  Pallas kernels  5.17 us (7%)
    all_to_all x1, blocking collectives, local(): exchanged = lax.all_to_all(packed, 'kring', 0, 0, axis_index_groups=[ring])  32 us
    all_to_all x1, blocking collectives, local(): lax.all_to_all(copies, orb, 0, 0, axis_index_groups=order)  19.1 us
    all_to_all x1, blocking collectives, local(): lax.all_to_all(tiles, near, 0, 0, axis_index_groups=members)  12 us
    pallas_call x1, Pallas kernels, pair_terms(): pl.pallas_call(lambda *refs: pair_kernel(virtuals, ring, *refs), out_shap...  2.13 us
    pallas_call x1, Pallas kernels, pack(): pl.pallas_call(pack_kernel, out_shape=(jax.ShapeDtypeStruct((contracted,...  1.98 us

profile of v10, /device:TPU:1, one launch (start us, length us, event | category | flops | bytes accessed | tf_op | source)
XLA Modules:
  0.0 68.6 jit_solution(2158878945052784286)
XLA Ops:
  0.0 2.0 %pack.1 = (bf16[896,896]{1,0:T(8,128)(2,1)S(1)}, s32[32,128]{1,0:T(8,128)S(1)}) custom-call(bf16[448,896]{1,0:T(8,128)(2,1)} %bitcast.12, bf16[448,896]{1,0:T(8,128)(2,1)} %bitcast.13, s32[32,32]{1,0:T(8,128)} %table_ref.1), custom_call_target="tpu_custom_call" | custom-call | tf_op jit(solution)/shard_map/pack/pallas_call | solution.py:61
  2.0 32.0 %all_to_all.15.refs_1_ = bf16[16,56,896]{2,1,0:T(8,128)(2,1)S(1)} all-to-all(bf16[16,56,896]{2,1,0:T(8,128)(2,1)S(1)} %bitcast.11), channel_id=1, replica_groups={{416,384,480,448,32,0,96,64,160,128,224,192,288,256,352,320},{417,385,4..., dimensions={0} | all-to-all | bytes 3211264 | tf_op jit(solution)/shard_map/all_to_all | solution.py:235
  34.0 0.0 copy-start
  34.0 2.1 %pairs.1 = f32[16,32,128]{2,1,0:T(8,128)S(1)} custom-call(s32[32,128]{1,0:T(8,128)S(1)} %get-tuple-element.7.refs_0_, bf16[16,56,896]{2,1,0:T(8,128)(2,1)S(1)} %all_to_all.15.refs_1_), custom_call_target="tpu_custom_call" | custom-call | tf_op jit(solution)/shard_map/pairs/pallas_call | solution.py:158
  36.2 12.0 %all_to_all.16 = f16[64,8,128]{2,1,0:T(8,128)(2,1)S(1)} all-to-all(f16[64,8,128]{2,1,0:T(8,128)(2,1)S(1)} %bitcast.14), channel_id=1, replica_groups={{416,417,432,433,384,385,400,401,480,481,496,497,448,449,464,465,32,33,..., dimensions={0} | all-to-all | bytes 262144 | tf_op jit(solution)/shard_map/all_to_all | solution.py:242
  48.2 0.1 multiply_exponential_fusion
  48.3 0.1 multiply_reduce_fusion
  48.4 19.1 %all_to_all.17 = f16[32,8,128]{2,1,0:T(8,128)(2,1)S(1)} all-to-all(f16[32,8,128]{2,1,0:T(8,128)(2,1)S(1)} %broadcast_in_dim.2), channel_id=1, replica_groups={{10,11,12,13,14,15,0,1,2,3,4,5,6,7,8,9,16,17,18,19,20,21,22,23,24,25,26..., dimensions={0} | all-to-all | bytes 131072 | tf_op jit(solution)/shard_map/all_to_all | solution.py:251
  67.5 0.0 copy-done
  67.5 1.1 %factors.1 = f32[2,7,2,1680]{3,2,1,0:T(2,128)} custom-call(f32[32,8,128]{2,1,0:T(8,128)S(1)} %convert_element_type.20.refs_0_, bf16[2,224,1680]{2,1,0:T(8,128)(2,1)S(1)} %bitcast.10), custom_call_target="tpu_custom_call" | custom-call | tf_op jit(solution)/shard_map/factors/pallas_call | solution.py:211
  (7 shorter events, 0.1 us)
Async XLA Ops:
  34.0 33.5 %copy-start = (bf16[2,2,112,1680]{3,2,1,0:T(8,128)(2,1)S(1)}, bf16[2,2,112,1680]{3,2,1,0:T(8,128)(2,1)}, u32[]{:S(2)}) copy-start(bf16[2,2,112,1680]{3,2,1,0:T(8,128)(2,1)} %param.6) | copy-start | bytes 4515844

commit v11 on v10

--- a/solution.py
+++ b/solution.py
@@ -177,17 +177,17 @@
     owned = out_ref.shape[1]
     virtuals = depth // 2
 
-    def unscaled(at):
-        part = parts_ref[at]
+    def unscaled(at, component):
+        part = parts_ref[at, component * SUBLANES : (component + 1) * SUBLANES]
         return part * jnp.exp2(part[owned : owned + 1] - SUM_HEADROOM)
 
     outgoing = []
     for q in range(qcount):
         density = []
         for component in range(2):
-            total = unscaled(q * far * 2 + component)
+            total = unscaled(q, component)
             for step in range(1, far):
-                total += unscaled((q * far + step) * 2 + component)
+                total += unscaled(step * qcount + q, component)
             density.append(total[:, :virtuals].astype(jnp.bfloat16).astype(jnp.float32))
         real, imag = density
         upper = jnp.concatenate([real, -imag], 1)
@@ -235,20 +235,25 @@
     exchanged = lax.all_to_all(packed, "kring", 0, 0, axis_index_groups=[ring])
     partial = pair_terms(slots, exchanged, virtuals, ring)
     near = ("kring", "y_lo", "z_lo")
-    orb = ("y_lo", "z_hi", "z_lo")
+    column = ("z_hi", "z_lo")
     pieces = lax.axis_size(near) // groups
     members = [[group * pieces + piece for group in ring for piece in range(pieces)]]
-    tiles = partial.reshape(lax.axis_size(near), SUBLANES, LANES).astype(jnp.float16)
+    height = 2 * SUBLANES
+    tiles = partial.astype(jnp.float16).reshape(groups, 1, qcount, height, LANES)
+    tiles = jnp.broadcast_to(tiles, (groups, pieces // qcount, qcount, height, LANES))
+    tiles = tiles.reshape(groups * pieces, height, LANES)
     tiles = lax.all_to_all(tiles, near, 0, 0, axis_index_groups=members).astype(jnp.float32)
     exponents = tiles[:, owned : owned + 1, :]
     largest = exponents.max(0)
     tile = (tiles * jnp.exp2(exponents - HEADROOM)).sum(0) * jnp.exp2(SUM_HEADROOM - largest)
-    tile = jnp.concatenate([tile[:owned], largest], 0).astype(jnp.float16)
-    copies = jnp.broadcast_to(tile[None], (lax.axis_size(orb),) + tile.shape)
-    depth = lax.axis_size(orb) // 2
+    second = SUBLANES + owned
+    tile = jnp.concatenate([tile[:owned], largest, tile[SUBLANES:second], largest], 0)
+    tile = tile.astype(jnp.float16)
+    depth = lax.axis_size(column)
+    copies = jnp.broadcast_to(tile[None], (depth,) + tile.shape)
     late = depth * 5 // 8
-    order = [[*range(late, depth), *range(late), *range(depth, 2 * depth)]]
-    parts = lax.all_to_all(copies, orb, 0, 0, axis_index_groups=order).astype(jnp.float32)
+    order = [[*range(late, depth), *range(late)]]
+    parts = lax.all_to_all(copies, column, 0, 0, axis_index_groups=order).astype(jnp.float32)
     factors = aux_factor.reshape(qcount, 2 * virtuals, aux_factor.shape[3])
     gamma = factor_product(parts, factors, owned, lax.axis_size("z_hi"))
     return gamma.transpose(0, 2, 1, 3)

time: 69 us -> 69.3 us (level)
    all_to_all x1, blocking collectives: 12 us -> 13.4 us  [local(): lax.all_to_all(tiles, near, 0, 0, axis_index_groups=members)]
    all_to_all x1, blocking collectives: 19.1 us -> 18 us  [local(): lax.all_to_all(copies, column, 0, 0, axis_index_groups=order)]
where the time goes in v11:
time: 69.3 us; the launch traced here: 69.1 us
  blocking collectives  63.5 us (92%)
  Pallas kernels  5.17 us (7%)
    all_to_all x1, blocking collectives, local(): exchanged = lax.all_to_all(packed, 'kring', 0, 0, axis_index_groups=[ring])  32 us
    all_to_all x1, blocking collectives, local(): lax.all_to_all(copies, column, 0, 0, axis_index_groups=order)  18 us
    all_to_all x1, blocking collectives, local(): lax.all_to_all(tiles, near, 0, 0, axis_index_groups=members)  13.4 us
    pallas_call x1, Pallas kernels, pair_terms(): pl.pallas_call(lambda *refs: pair_kernel(virtuals, ring, *refs), out_shap...  2.13 us
    pallas_call x1, Pallas kernels, pack(): pl.pallas_call(pack_kernel, out_shape=(jax.ShapeDtypeStruct((contracted,...  1.98 us

profile of v11, /device:TPU:1, one launch (start us, length us, event | category | flops | bytes accessed | tf_op | source)
XLA Modules:
  0.0 69.1 jit_solution(1689440893941478263)
XLA Ops:
  0.0 2.0 %pack.1 = (bf16[896,896]{1,0:T(8,128)(2,1)S(1)}, s32[32,128]{1,0:T(8,128)S(1)}) custom-call(bf16[448,896]{1,0:T(8,128)(2,1)} %bitcast.14, bf16[448,896]{1,0:T(8,128)(2,1)} %bitcast.15, s32[32,32]{1,0:T(8,128)} %table_ref.1), custom_call_target="tpu_custom_call" | custom-call | tf_op jit(solution)/shard_map/pack/pallas_call | solution.py:61
  2.0 32.0 %all_to_all.15.refs_1_ = bf16[16,56,896]{2,1,0:T(8,128)(2,1)S(1)} all-to-all(bf16[16,56,896]{2,1,0:T(8,128)(2,1)S(1)} %bitcast.12), channel_id=1, replica_groups={{416,384,480,448,32,0,96,64,160,128,224,192,288,256,352,320},{417,385,4..., dimensions={0} | all-to-all | bytes 3211264 | tf_op jit(solution)/shard_map/all_to_all | solution.py:235
  34.0 2.1 %pairs.1 = f32[16,32,128]{2,1,0:T(8,128)S(1)} custom-call(s32[32,128]{1,0:T(8,128)S(1)} %get-tuple-element.7.refs_0_, bf16[16,56,896]{2,1,0:T(8,128)(2,1)S(1)} %all_to_all.15.refs_1_), custom_call_target="tpu_custom_call" | custom-call | tf_op jit(solution)/shard_map/pairs/pallas_call | solution.py:158
  36.2 0.0 copy-start
  36.3 13.4 %all_to_all.16 = f16[64,16,128]{2,1,0:T(8,128)(2,1)S(1)} all-to-all(f16[64,16,128]{2,1,0:T(8,128)(2,1)S(1)} %bitcast.13), channel_id=1, replica_groups={{416,417,432,433,384,385,400,401,480,481,496,497,448,449,464,465,32,33,..., dimensions={0} | all-to-all | bytes 524288 | tf_op jit(solution)/shard_map/all_to_all | solution.py:245
  49.7 0.1 multiply_exponential_fusion
  49.8 0.1 multiply_reduce_fusion
  50.0 18.0 %all_to_all.17 = f16[16,16,128]{2,1,0:T(8,128)(2,1)S(1)} all-to-all(f16[16,16,128]{2,1,0:T(8,128)(2,1)S(1)} %broadcast_in_dim.15), channel_id=1, replica_groups={{10,11,12,13,14,15,0,1,2,3,4,5,6,7,8,9},{26,27,28,29,30,31,16,17,18,19,..., dimensions={0} | all-to-all | bytes 131072 | tf_op jit(solution)/shard_map/all_to_all | solution.py:256
  68.0 0.0 copy-done
  68.0 1.1 %factors.1 = f32[2,7,2,1680]{3,2,1,0:T(2,128)} custom-call(f32[16,16,128]{2,1,0:T(8,128)S(1)} %convert_element_type.16.refs_0_, bf16[2,224,1680]{2,1,0:T(8,128)(2,1)S(1)} %bitcast.11), custom_call_target="tpu_custom_call" | custom-call | tf_op jit(solution)/shard_map/factors/pallas_call | solution.py:211
  (10 shorter events, 0.2 us)
Async XLA Ops:
  36.2 31.8 %copy-start = (bf16[2,2,112,1680]{3,2,1,0:T(8,128)(2,1)S(1)}, bf16[2,2,112,1680]{3,2,1,0:T(8,128)(2,1)}, u32[]{:S(2)}) copy-start(bf16[2,2,112,1680]{3,2,1,0:T(8,128)(2,1)} %param.6) | copy-start | bytes 4515844

commit v12 on v10

--- a/solution.py
+++ b/solution.py
@@ -116,18 +116,20 @@
                 transfer == q, value, jnp.zeros_like(value)
             )
 
-    for triple in range(triples):
-        choose(0, triple)
-        choose(1, triple)
-    tau_all = tau_part[...].reshape(triples * slot_rows, 2 * virtuals)
     wide = qcount * 2 * LANES
-    products = lax.dot_general(
-        tau_all,
-        chosen[...].reshape(triples * slot_rows, 2 * wide),
-        (((0,), (0,)), ((), ())),
-        preferred_element_type=jnp.float32,
-    )
-    total = products[:, :wide] + products[:, wide:]
+    total = jnp.zeros((2 * virtuals, wide), jnp.float32)
+    part = triples // 2
+    for first in range(0, triples, part):
+        for triple in range(first, first + part):
+            choose(0, triple)
+            choose(1, triple)
+        products = lax.dot_general(
+            tau_part[first : first + part].reshape(part * slot_rows, 2 * virtuals),
+            chosen[first : first + part].reshape(part * slot_rows, 2 * wide),
+            (((0,), (0,)), ((), ())),
+            preferred_element_type=jnp.float32,
+        )
+        total += products[:, :wide] + products[:, wide:]
     owned = virtuals // groups
     pieces = []
     for q in range(qcount):

time: 69 us -> 69 us (level)
  no operation moved by 1% of the time
where the time goes in v12:
time: 69 us; the launch traced here: 68.6 us
  blocking collectives  63.1 us (91%)
  Pallas kernels  5.17 us (7%)
    all_to_all x1, blocking collectives, local(): exchanged = lax.all_to_all(packed, 'kring', 0, 0, axis_index_groups=[ring])  32 us
    all_to_all x1, blocking collectives, local(): lax.all_to_all(copies, orb, 0, 0, axis_index_groups=order)  19.1 us
    all_to_all x1, blocking collectives, local(): lax.all_to_all(tiles, near, 0, 0, axis_index_groups=members)  12 us
    pallas_call x1, Pallas kernels, pair_terms(): pl.pallas_call(lambda *refs: pair_kernel(virtuals, ring, *refs), out_shap...  2.13 us
    pallas_call x1, Pallas kernels, pack(): pl.pallas_call(pack_kernel, out_shape=(jax.ShapeDtypeStruct((contracted,...  1.98 us

profile of v12, /device:TPU:1, one launch (start us, length us, event | category | flops | bytes accessed | tf_op | source)
XLA Modules:
  0.0 68.6 jit_solution(2613467203029479478)
XLA Ops:
  0.0 2.0 %pack.1 = (bf16[896,896]{1,0:T(8,128)(2,1)S(1)}, s32[32,128]{1,0:T(8,128)S(1)}) custom-call(bf16[448,896]{1,0:T(8,128)(2,1)} %bitcast.12, bf16[448,896]{1,0:T(8,128)(2,1)} %bitcast.13, s32[32,32]{1,0:T(8,128)} %table_ref.1), custom_call_target="tpu_custom_call" | custom-call | tf_op jit(solution)/shard_map/pack/pallas_call | solution.py:61
  2.0 32.0 %all_to_all.15.refs_1_ = bf16[16,56,896]{2,1,0:T(8,128)(2,1)S(1)} all-to-all(bf16[16,56,896]{2,1,0:T(8,128)(2,1)S(1)} %bitcast.11), channel_id=1, replica_groups={{416,384,480,448,32,0,96,64,160,128,224,192,288,256,352,320},{417,385,4..., dimensions={0} | all-to-all | bytes 3211264 | tf_op jit(solution)/shard_map/all_to_all | solution.py:237
  34.0 0.0 copy-start
  34.0 2.1 %pairs.1 = f32[16,32,128]{2,1,0:T(8,128)S(1)} custom-call(s32[32,128]{1,0:T(8,128)S(1)} %get-tuple-element.7.refs_0_, bf16[16,56,896]{2,1,0:T(8,128)(2,1)S(1)} %all_to_all.15.refs_1_), custom_call_target="tpu_custom_call" | custom-call | tf_op jit(solution)/shard_map/pairs/pallas_call | solution.py:160
  36.2 12.0 %all_to_all.16 = f16[64,8,128]{2,1,0:T(8,128)(2,1)S(1)} all-to-all(f16[64,8,128]{2,1,0:T(8,128)(2,1)S(1)} %bitcast.14), channel_id=1, replica_groups={{416,417,432,433,384,385,400,401,480,481,496,497,448,449,464,465,32,33,..., dimensions={0} | all-to-all | bytes 262144 | tf_op jit(solution)/shard_map/all_to_all | solution.py:244
  48.2 0.1 multiply_exponential_fusion
  48.3 0.1 multiply_reduce_fusion
  48.4 19.1 %all_to_all.17 = f16[32,8,128]{2,1,0:T(8,128)(2,1)S(1)} all-to-all(f16[32,8,128]{2,1,0:T(8,128)(2,1)S(1)} %broadcast_in_dim.2), channel_id=1, replica_groups={{10,11,12,13,14,15,0,1,2,3,4,5,6,7,8,9,16,17,18,19,20,21,22,23,24,25,26..., dimensions={0} | all-to-all | bytes 131072 | tf_op jit(solution)/shard_map/all_to_all | solution.py:253
  67.5 0.0 copy-done
  67.5 1.1 %factors.1 = f32[2,7,2,1680]{3,2,1,0:T(2,128)} custom-call(f32[32,8,128]{2,1,0:T(8,128)S(1)} %convert_element_type.20.refs_0_, bf16[2,224,1680]{2,1,0:T(8,128)(2,1)S(1)} %bitcast.10), custom_call_target="tpu_custom_call" | custom-call | tf_op jit(solution)/shard_map/factors/pallas_call | solution.py:213
  (7 shorter events, 0.1 us)
Async XLA Ops:
  34.0 33.5 %copy-start = (bf16[2,2,112,1680]{3,2,1,0:T(8,128)(2,1)S(1)}, bf16[2,2,112,1680]{3,2,1,0:T(8,128)(2,1)}, u32[]{:S(2)}) copy-start(bf16[2,2,112,1680]{3,2,1,0:T(8,128)(2,1)} %param.6) | copy-start | bytes 4515844

commit v13 on v10

--- a/solution.py
+++ b/solution.py
@@ -47,12 +47,12 @@
             )
     for copy in incoming:
         copy.start()
-    table_copy.wait()
-    slots_ref[...] = partner_slots(table_here[...], slots_ref.shape)
     for tile in range(tiles):
         incoming[2 * tile].wait()
         incoming[2 * tile + 1].wait()
         packed_ref[tile * LANES : (tile + 1) * LANES] = both[tile].T
+    table_copy.wait()
+    slots_ref[...] = partner_slots(table_here[...], slots_ref.shape)
 
 
 def pack(tau_rows, lambda_rows, table):

time: 69 us -> 69.2 us (level)
  no operation moved by 1% of the time
where the time goes in v13:
time: 69.2 us; the launch traced here: 68.8 us
  blocking collectives  63.1 us (91%)
  Pallas kernels  5.43 us (8%)
    all_to_all x1, blocking collectives, local(): exchanged = lax.all_to_all(packed, 'kring', 0, 0, axis_index_groups=[ring])  32 us
    all_to_all x1, blocking collectives, local(): lax.all_to_all(copies, orb, 0, 0, axis_index_groups=order)  19.1 us
    all_to_all x1, blocking collectives, local(): lax.all_to_all(tiles, near, 0, 0, axis_index_groups=members)  12 us
    pallas_call x1, Pallas kernels, pack(): pl.pallas_call(pack_kernel, out_shape=(jax.ShapeDtypeStruct((contracted,...  2.23 us
    pallas_call x1, Pallas kernels, pair_terms(): pl.pallas_call(lambda *refs: pair_kernel(virtuals, ring, *refs), out_shap...  2.13 us

profile of v13, /device:TPU:1, one launch (start us, length us, event | category | flops | bytes accessed | tf_op | source)
XLA Modules:
  0.0 68.8 jit_solution(50389481272698456)
XLA Ops:
  0.0 2.2 %pack.1 = (bf16[896,896]{1,0:T(8,128)(2,1)S(1)}, s32[32,128]{1,0:T(8,128)S(1)}) custom-call(bf16[448,896]{1,0:T(8,128)(2,1)} %bitcast.12, bf16[448,896]{1,0:T(8,128)(2,1)} %bitcast.13, s32[32,32]{1,0:T(8,128)} %table_ref.1), custom_call_target="tpu_custom_call" | custom-call | tf_op jit(solution)/shard_map/pack/pallas_call | solution.py:61
  2.2 32.0 %all_to_all.15.refs_1_ = bf16[16,56,896]{2,1,0:T(8,128)(2,1)S(1)} all-to-all(bf16[16,56,896]{2,1,0:T(8,128)(2,1)S(1)} %bitcast.11), channel_id=1, replica_groups={{416,384,480,448,32,0,96,64,160,128,224,192,288,256,352,320},{417,385,4..., dimensions={0} | all-to-all | bytes 3211264 | tf_op jit(solution)/shard_map/all_to_all | solution.py:235
  34.3 0.0 copy-start
  34.3 2.1 %pairs.1 = f32[16,32,128]{2,1,0:T(8,128)S(1)} custom-call(s32[32,128]{1,0:T(8,128)S(1)} %get-tuple-element.7.refs_0_, bf16[16,56,896]{2,1,0:T(8,128)(2,1)S(1)} %all_to_all.15.refs_1_), custom_call_target="tpu_custom_call" | custom-call | tf_op jit(solution)/shard_map/pairs/pallas_call | solution.py:158
  36.5 12.0 %all_to_all.16 = f16[64,8,128]{2,1,0:T(8,128)(2,1)S(1)} all-to-all(f16[64,8,128]{2,1,0:T(8,128)(2,1)S(1)} %bitcast.14), channel_id=1, replica_groups={{416,417,432,433,384,385,400,401,480,481,496,497,448,449,464,465,32,33,..., dimensions={0} | all-to-all | bytes 262144 | tf_op jit(solution)/shard_map/all_to_all | solution.py:242
  48.5 0.1 multiply_exponential_fusion
  48.6 0.1 multiply_reduce_fusion
  48.7 19.1 %all_to_all.17 = f16[32,8,128]{2,1,0:T(8,128)(2,1)S(1)} all-to-all(f16[32,8,128]{2,1,0:T(8,128)(2,1)S(1)} %broadcast_in_dim.2), channel_id=1, replica_groups={{10,11,12,13,14,15,0,1,2,3,4,5,6,7,8,9,16,17,18,19,20,21,22,23,24,25,26..., dimensions={0} | all-to-all | bytes 131072 | tf_op jit(solution)/shard_map/all_to_all | solution.py:251
  67.8 0.0 copy-done
  67.8 1.1 %factors.1 = f32[2,7,2,1680]{3,2,1,0:T(2,128)} custom-call(f32[32,8,128]{2,1,0:T(8,128)S(1)} %convert_element_type.20.refs_0_, bf16[2,224,1680]{2,1,0:T(8,128)(2,1)S(1)} %bitcast.10), custom_call_target="tpu_custom_call" | custom-call | tf_op jit(solution)/shard_map/factors/pallas_call | solution.py:211
  (7 shorter events, 0.1 us)
Async XLA Ops:
  34.3 33.5 %copy-start = (bf16[2,2,112,1680]{3,2,1,0:T(8,128)(2,1)S(1)}, bf16[2,2,112,1680]{3,2,1,0:T(8,128)(2,1)}, u32[]{:S(2)}) copy-start(bf16[2,2,112,1680]{3,2,1,0:T(8,128)(2,1)} %param.6) | copy-start | bytes 4515844
